TPU v7x, 128 devices: a whole 4x4x4 slice. The times are simulated.
128 devices in a mesh: row: 8 (over y, core), col: 16 (over x, z).
Axes of the slice: x: 4, y: 4, z: 4, core: 2. Of those that a mesh axis runs over, the one named last changes fastest.
Arguments:
- front: float32 [8, 16, 128, 16, 8, 128], P('row', None, None, 'col'), may hold values from -1 to 3, as said below
- children: bfloat16 [8, 24, 128, 16, 6, 128], P('row', None, None, 'col'), may hold values from -8 to 14, as said below
- child_maps: int32 [2, 96], replicated, may hold values from 0 to 127, as said below
- fill: int32 [128, 128], replicated, may hold values from 0 to 1, as said below
Outputs:
- factored: float32 [8, 16, 128, 16, 8, 128], P('row', None, None, 'col')
Inputs may be any that keep to these rules, and one draw needn't show every extreme that they name: `front`: symmetric positive definite. `children`: each child's matrix is symmetric positive definite. `child_maps`: A row's 96 entries are distinct. For each group g, the child tiles g * 16 to (g + 1) * 16 - 1 go, as a cyclic shift, onto one aligned block of 16 parent tiles; in each row one group goes onto the parent tiles 0 to 15. The child tiles that one device holds send at most 1 tile columns to one column of the grid and at most 4 tile rows to one row of the grid, and devices reach both bounds. `fill`: symmetric, with ones on the diagonal.
All inputs are finite; a program needn't handle non-finite values.
Results may differ from a plain program's by a relative error of at most 0.0003.
Values may be sent and summed in bfloat16 or wider, within the bound.
A program may use at most 192 MiB of HBM per device.

v0:
```python
import jax
import jax.numpy as jnp
from jax import lax
from jax.sharding import PartitionSpec as P

PT = 4
PANELS = 3


def from_root(array, axis, root):
    mine = lax.axis_index(axis) == root
    return lax.psum(jnp.where(mine, array, jnp.zeros_like(array)), axis)


def ranked(targets):
    positions = jnp.arange(targets.shape[0])
    earlier = (targets[None, :] == targets[:, None]) & (positions[None, :] < positions[:, None])
    return jnp.sum(earlier.astype(jnp.int32), axis=1)


def select_slots(targets, places, capacity):
    rank_of = ranked(targets)
    matches = (targets[None, None, :] == jnp.arange(places)[:, None, None]) & (
        rank_of[None, None, :] == jnp.arange(capacity)[None, :, None]
    )
    return (jnp.argmax(matches, axis=-1), jnp.any(matches, axis=-1))


def local(front, children, child_maps, fill):
    n_row = lax.axis_size("row")
    n_col = lax.axis_size("col")
    half_rows = n_row // 2
    row_id = lax.axis_index("row")
    col_id = lax.axis_index("col")
    child_tiles = children[0, :, :, 0]
    child_rows = child_tiles.shape[0]
    tile_size = child_tiles.shape[1]
    groups = child_tiles.shape[2]
    parent_rows = front.shape[1]
    parent_cols = front.shape[4]
    per_class = n_col // half_rows
    cap_col = ((groups + half_rows - 1) // half_rows + per_class - 1) // per_class
    cap_row = n_col // n_row * ((groups + half_rows - 1) // half_rows)
    maps_cols = child_maps.reshape(2, groups, n_col)
    maps_rows = child_maps.reshape(2, child_rows, half_rows)
    own_child = row_id // half_rows
    own_lane = row_id % half_rows
    my_col_maps = maps_cols[own_child][:, col_id]
    my_row_maps = maps_rows[own_child][:, own_lane]

    def column_sources(col_maps):
        slot_picks, valids = jax.vmap(
            lambda source_maps: select_slots(source_maps, n_col, cap_col), in_axes=1
        )(col_maps % n_col)
        own_slots = slot_picks[:, col_id]
        own_valid = valids[:, col_id]
        sources = jnp.arange(n_col)[:, None]
        tile_cols = col_maps[own_slots, sources] // n_col
        hit_table = (
            own_slots.reshape(-1)[None, :] == jnp.arange(groups)[:, None]
        ) & own_valid.reshape(-1)[None, :]
        flat_slots = jnp.argmax(hit_table, axis=1)
        ordered = col_maps[jnp.arange(groups), flat_slots // cap_col] // n_col
        return (tile_cols, own_valid, flat_slots, ordered)

    src_cols, src_valid, flat_order, ordered_cols = jax.vmap(column_sources)(maps_cols)

    def row_sources(source_row):
        row_maps = maps_rows[source_row // half_rows][:, source_row % half_rows]
        slot_picks, valids = select_slots(row_maps % n_row, n_row, cap_row)
        own_slots = slot_picks[row_id]
        return jnp.where(valids[row_id], row_maps[own_slots] // n_row, parent_rows)

    row_targets = jax.vmap(row_sources)(jnp.arange(n_row))
    row_send, row_flags = select_slots(my_row_maps % n_row, n_row, cap_row)
    col_send, col_flags = select_slots(my_col_maps % n_col, n_col, cap_col)
    extend = jnp.zeros((parent_rows, tile_size, parent_cols, tile_size), jnp.float32)
    col_buffer = jnp.take(child_tiles, col_send.reshape(-1), axis=2).reshape(
        child_rows, tile_size, n_col, cap_col, tile_size
    )
    arrived = lax.all_to_all(col_buffer, "col", split_axis=2, concat_axis=2, tiled=True)
    compact = jnp.take(
        arrived.reshape(child_rows, tile_size, n_col * cap_col, tile_size),
        flat_order[own_child],
        axis=2,
    )
    row_buffer = jnp.take(compact, row_send.reshape(-1), axis=0).reshape(
        n_row, cap_row, tile_size, groups, tile_size
    )
    received = lax.all_to_all(row_buffer, "row", split_axis=0, concat_axis=0, tiled=True)
    col_targets = ordered_cols[jnp.arange(n_row) // half_rows]
    values = received.transpose(0, 1, 3, 2, 4).astype(jnp.float32)
    extend = extend.at[row_targets[:, :, None], :, col_targets[:, None, :], :].add(
        values, mode="drop"
    )
    fill_rows = lax.dynamic_index_in_dim(
        fill.reshape(parent_rows, n_row, parent_cols, n_col), row_id, 1, keepdims=False
    )
    fill_local = lax.dynamic_index_in_dim(fill_rows, col_id, 2, keepdims=False).astype(jnp.float32)
    parent = front[0, :, :, 0] * fill_local[:, None, :, None] + extend
    row_tiles = row_id + n_row * jnp.arange(parent_rows)
    col_tiles = col_id + n_col * jnp.arange(parent_cols)
    width = PT * tile_size
    stride = n_col // n_row
    for panel_index in range(PANELS):
        first_tile = panel_index * PT
        pieces = []
        for offset in range(PT):
            tile_index = first_tile + offset
            pieces.append(
                from_root(parent[:, :, tile_index // n_col, :], "col", tile_index % n_col)
            )
        panel_strip = jnp.stack(pieces, axis=2).reshape(parent_rows * tile_size, width)
        blocks = []
        for offset in range(PT):
            tile_index = first_tile + offset
            owner = row_id == tile_index % n_row
            local_row = tile_index // n_row
            blocks.append(
                jnp.where(
                    owner, panel_strip[local_row * tile_size : (local_row + 1) * tile_size], 0.0
                )
            )
        diagonal_block = lax.psum(jnp.concatenate(blocks, axis=0), "row")
        diag_factor = jnp.linalg.cholesky(diagonal_block)
        solved = lax.linalg.triangular_solve(
            diag_factor, panel_strip, left_side=False, lower=True, transpose_a=True
        )
        solved = solved.reshape(parent_rows, tile_size, width)
        solved = jnp.where((row_tiles >= first_tile)[:, None, None], solved, 0.0)
        factor_tiles = diag_factor.reshape(PT, tile_size, width)
        for offset in range(PT):
            solved = jnp.where(
                (row_tiles == first_tile + offset)[:, None, None], factor_tiles[offset], solved
            )
        for offset in range(PT):
            tile_index = first_tile + offset
            owner = col_id == tile_index % n_col
            local_col = tile_index // n_col
            current = parent[:, :, local_col, :]
            parent = parent.at[:, :, local_col, :].set(
                jnp.where(
                    owner, solved[:, :, offset * tile_size : (offset + 1) * tile_size], current
                )
            )
        needed = lax.dynamic_index_in_dim(
            solved.reshape(parent_cols, stride, tile_size, width),
            col_id // n_row,
            1,
            keepdims=False,
        )
        col_factors = from_root(needed, "row", col_id % n_row)
        update = jnp.dot(
            solved.reshape(parent_rows * tile_size, width),
            col_factors.reshape(parent_cols * tile_size, width).T,
            precision=lax.Precision.HIGHEST,
            preferred_element_type=jnp.float32,
        )
        update = update.reshape(parent_rows, tile_size, parent_cols, tile_size)
        after_tile = first_tile + PT
        keep_mask = (row_tiles >= after_tile)[:, None] & (col_tiles >= after_tile)[None, :]
        parent = parent - jnp.where(keep_mask[:, None, :, None], update, 0.0)
    finished = PANELS * PT
    upper_mask = (row_tiles < finished)[:, None] & (col_tiles >= finished)[None, :]
    parent = jnp.where(upper_mask[:, None, :, None], 0.0, parent)
    return parent.reshape(1, parent_rows, tile_size, 1, parent_cols, tile_size)


def solution(mesh):
    placed = (
        P("row", None, None, "col", None, None),
        P("row", None, None, "col", None, None),
        P(),
        P(),
    )
    return jax.shard_map(
        local,
        mesh=mesh,
        in_specs=placed,
        out_specs=P("row", None, None, "col", None, None),
        check_vma=False,
    )
```

profile of v0, /device:TPU:0, one launch (start us, length us, event | category | flops | bytes accessed | tf_op | source)
XLA Modules:
  0.0 1933.3 jit_solution(14672942148556759082)
XLA Ops:
  8.4 8.6 gather_fusion.2
  17.0 10.8 bitcast_select_fusion
  27.8 8.1 all-to-all-start
  47.4 204.9 %all-to-all-done = bf16[24,128,16,1,128]{4,1,0,3,2:T(8,128)(2,1)} async-done(((bf16[24,128,16,1,128]{4,1,0,3,2:T(8,128)(2,1)}), bf16[24,128,16,1,128]{4,1,0,3,2:T(8,128)(2,1)}, u32[]{:S(2)}, u32[]{:S(2)}) %all-to-all-start) | async-done | bytes 12582944 | tf_op jit(solution)/shard_map/all_to_all | solution.py:81
  252.3 8.1 gather_fusion.3
  265.4 6.4 gather_fusion.4
  271.8 6.1 broadcast_select_fusion
  285.7 8.9 bitcast_multiply_fusion
  294.6 60.4 %all-to-all-done.1 = bf16[8,4,128,6,128]{4,2,3,1,0:T(8,128)(2,1)} async-done(((bf16[8,4,128,6,128]{4,2,3,1,0:T(8,128)(2,1)}), bf16[8,4,128,6,128]{4,2,3,1,0:T(8,128)(2,1)}, u32[]{:S(2)}, u32[]{:S(2)}) %all-to-all-start.1) | async-done | bytes 6291488 | tf_op jit(solution)/shard_map/all_to_all | solution.py:90
  354.9 8.9 convert_element_type.29
  363.8 40.2 %scatter_fusion = f32[16,128,8,128]{3,1,2,0:T(8,128)} fusion(f32[16,128,8,128]{3,1,2,0:T(8,128)} %bitcast_multiply_fusion, s32[192]{0:T(256)S(1)} %reshape.1633, f32[192,128,128]{2,1,0:T(8,128)} %bitcast.442), kind=kCustom, calls=%fused_computation.8 | custom fusion | flops 3145728 | bytes 37750272 | tf_op jit(solution)/shard_map/scatter-add | solution.py:93
  408.2 110.2 %all-reduce.32.cloned.1.call-done = (f32[16,128,1,128]{3,1,0,2:T(8,128)}, f32[16,128,1,128]{3,1,0,2:T(8,128)}, f32[16,128,1,128]{3,1,0,2:T(8,128)}, f32[16,128,1,128]{3,1,0,2:T(8,128)}) async-done(((f32[16,128,1,128]{3,1,0,2:T(8,128)}, f32[16,128,1,128]{3,1,0,2:T(8,128)}, f32[16,128,1,128]{3,1,0,2:T(8,128)}, f32[16,128,1,128]{3,1,0,2:T(8,128)}), (f32[16,128,1,128]{3,1,0,2:T(8,128)}, ...) | async-done | bytes 4194320 | tf_op jit(solution)/shard_map/psum | solution.py:12
  525.3 5.4 copy.522
  544.6 51.1 %all-reduce.16.cloned.1.call-done = f32[512,512]{0,1:T(8,128)} async-done(((f32[512,512]{0,1:T(8,128)}), f32[512,512]{0,1:T(8,128)}) %all-reduce.16.cloned.1.call-update) | async-done | bytes 1048592 | tf_op jit(solution)/shard_map/psum | solution.py:124
  599.7 11.7 cholesky.374
  611.6 9.8 custom-call.41
  624.0 11.9 cholesky.393
  637.2 9.8 custom-call.42
  648.6 11.7 cholesky.414
  661.0 9.8 custom-call.43
  672.3 12.1 cholesky.431
  689.2 11.8 while.22
  701.0 39.3 %custom-call.44 = f32[4,128,128]{1,2,0:T(8,128)S(1)} custom-call(f32[4,128,128]{2,1,0:T(8,128)S(1)} %get-tuple-element.225), custom_call_target="InvertDiagBlocksLowerTriangular" | custom-call | tf_op jit(solution)/shard_map/triangular_solve/custom-call.3 | solution.py:126
  751.9 6.6 fusion.24
  781.6 5.4 copy.585
  795.8 9.7 select_select_fusion.4
  805.5 6.6 reshape.1422
  851.8 43.1 %all-reduce.18.cloned.1.call-done = f32[8,128,512]{2,1,0:T(8,128)} async-done(((f32[8,128,512]{2,1,0:T(8,128)}), f32[8,128,512]{2,1,0:T(8,128)}) %all-reduce.18.cloned.1.call-update) | async-done | bytes 2097168 | tf_op jit(solution)/shard_map/psum | solution.py:12
  895.0 17.2 select_subtract_fusion.1
  918.4 103.2 %all-reduce.30.cloned.1.call-done = (f32[16,128,1,128]{3,1,0,2:T(8,128)}, f32[16,128,1,128]{3,1,0,2:T(8,128)}, f32[16,128,1,128]{3,1,0,2:T(8,128)}, f32[16,128,1,128]{3,1,0,2:T(8,128)}) async-done(((f32[16,128,1,128]{3,1,0,2:T(8,128)}, f32[16,128,1,128]{3,1,0,2:T(8,128)}, f32[16,128,1,128]{3,1,0,2:T(8,128)}, f32[16,128,1,128]{3,1,0,2:T(8,128)}), (f32[16,128,1,128]{3,1,0,2:T(8,128)}, ...) | async-done | bytes 4194320 | tf_op jit(solution)/shard_map/psum | solution.py:12
  1028.6 5.4 copy.543
  1047.7 51.3 %all-reduce.20.cloned.1.call-done = f32[512,512]{0,1:T(8,128)} async-done(((f32[512,512]{0,1:T(8,128)}), f32[512,512]{0,1:T(8,128)}) %all-reduce.20.cloned.1.call-update) | async-done | bytes 1048592 | tf_op jit(solution)/shard_map/psum | solution.py:124
  1103.0 11.7 cholesky.446
  1114.9 9.8 custom-call.45
  1127.2 11.9 cholesky.465
  1140.4 9.8 custom-call.46
  1151.8 11.7 cholesky.486
  1164.3 9.8 custom-call.47
  1175.5 12.1 cholesky.503
  1192.5 11.8 while.23
  1204.2 39.3 %custom-call.48 = f32[4,128,128]{1,2,0:T(8,128)S(1)} custom-call(f32[4,128,128]{2,1,0:T(8,128)S(1)} %get-tuple-element.226), custom_call_target="InvertDiagBlocksLowerTriangular" | custom-call | tf_op jit(solution)/shard_map/triangular_solve/custom-call.3 | solution.py:126
  1255.1 6.6 fusion.21
  1299.1 9.7 select_select_fusion.2
  1308.8 6.6 reshape.1426
  1355.1 43.1 %all-reduce.22.cloned.1.call-done = f32[8,128,512]{2,1,0:T(8,128)} async-done(((f32[8,128,512]{2,1,0:T(8,128)}), f32[8,128,512]{2,1,0:T(8,128)}) %all-reduce.22.cloned.1.call-update) | async-done | bytes 2097168 | tf_op jit(solution)/shard_map/psum | solution.py:12
  1398.2 17.2 select_subtract_fusion
  1421.6 103.2 %all-reduce.28.cloned.1.call-done = (f32[16,128,1,128]{3,1,0,2:T(8,128)}, f32[16,128,1,128]{3,1,0,2:T(8,128)}, f32[16,128,1,128]{3,1,0,2:T(8,128)}, f32[16,128,1,128]{3,1,0,2:T(8,128)}) async-done(((f32[16,128,1,128]{3,1,0,2:T(8,128)}, f32[16,128,1,128]{3,1,0,2:T(8,128)}, f32[16,128,1,128]{3,1,0,2:T(8,128)}, f32[16,128,1,128]{3,1,0,2:T(8,128)}), (f32[16,128,1,128]{3,1,0,2:T(8,128)}, ...) | async-done | bytes 4194320 | tf_op jit(solution)/shard_map/psum | solution.py:12
  1529.9 5.4 copy.564
  1548.0 51.3 %all-reduce.24.cloned.1.call-done = f32[512,512]{0,1:T(8,128)} async-done(((f32[512,512]{0,1:T(8,128)}), f32[512,512]{0,1:T(8,128)}) %all-reduce.24.cloned.1.call-update) | async-done | bytes 1048592 | tf_op jit(solution)/shard_map/psum | solution.py:124
  1603.3 11.7 cholesky.518
  1615.2 9.8 custom-call.49
  1627.5 11.9 cholesky.537
  1640.8 9.8 custom-call.50
  1652.1 11.7 cholesky.558
  1664.6 9.8 custom-call.51
  1675.8 12.1 cholesky.575
  1692.8 11.8 while.24
  1704.6 39.3 %custom-call.52 = f32[4,128,128]{1,2,0:T(8,128)S(1)} custom-call(f32[4,128,128]{2,1,0:T(8,128)S(1)} %get-tuple-element.227), custom_call_target="InvertDiagBlocksLowerTriangular" | custom-call | tf_op jit(solution)/shard_map/triangular_solve/custom-call.3 | solution.py:126
  1755.5 6.6 fusion.18
  1799.4 9.7 select_select_fusion
  1809.1 6.6 reshape.1430
  1855.2 43.5 %all-reduce.26.cloned.1.call-done = f32[8,128,512]{2,1,0:T(8,128)} async-done(((f32[8,128,512]{2,1,0:T(8,128)}), f32[8,128,512]{2,1,0:T(8,128)}) %all-reduce.26.cloned.1.call-update) | async-done | bytes 2097168 | tf_op jit(solution)/shard_map/psum | solution.py:12
  1898.7 17.8 select_bitcast_fusion
  1916.5 9.9 copy.578
  (456 shorter events, 438.3 us)
Async XLA Ops:
  27.8 8.2 copy-start.34
  27.8 224.6 %all-to-all-start = ((bf16[24,128,16,1,128]{4,1,0,3,2:T(8,128)(2,1)}), bf16[24,128,16,1,128]{4,1,0,3,2:T(8,128)(2,1)}, u32[]{:S(2)}, u32[]{:S(2)}) async-start(bf16[24,128,16,1,128]{4,1,0,3,2:T(8,128)(2,1)} %bitcast_select_fusion), calls=%async_computation | async-start | bytes 25165824 | tf_op jit(solution)/shard_map/all_to_all | solution.py:81
  277.9 7.3 copy-start.33
  277.9 77.1 %all-to-all-start.1 = ((bf16[8,4,128,6,128]{4,2,3,1,0:T(8,128)(2,1)}), bf16[8,4,128,6,128]{4,2,3,1,0:T(8,128)(2,1)}, u32[]{:S(2)}, u32[]{:S(2)}) async-start(bf16[8,4,128,6,128]{4,2,3,1,0:T(8,128)(2,1)} %broadcast_select_fusion), calls=%async_computation.1 | async-start | bytes 12582912 | tf_op jit(solution)/shard_map/all_to_all | solution.py:90
  282.8 235.5 %all-reduce.32.cloned.1.call-start = ((), (), s32[]{:S(2)}) async-start(), calls=%async_computation.10 | async-start | bytes 8388608 | tf_op jit(solution)/shard_map/psum | solution.py:12
  407.4 188.3 %all-reduce.16.cloned.1.call-start = ((), (), s32[]{:S(2)}) async-start(), calls=%async_computation.2 | async-start | bytes 2097152 | tf_op jit(solution)/shard_map/psum | solution.py:124
  518.3 4.8 copy-start.28
  518.3 5.9 copy-start.27
  533.4 361.5 %all-reduce.18.cloned.1.call-start = ((), (), s32[]{:S(2)}) async-start(), calls=%async_computation.3 | async-start | bytes 4194304 | tf_op jit(solution)/shard_map/psum | solution.py:12
  538.1 1.9 copy-start.6
  598.7 1.0 copy-start.24
  745.2 6.6 copy-start.13
  751.9 8.6 copy-start.10
  817.5 10.0 copy-start.15
  817.5 10.0 copy-start.16
  817.5 10.0 copy-start.17
  829.8 191.8 %all-reduce.30.cloned.1.call-start = ((), (), s32[]{:S(2)}) async-start(), calls=%async_computation.9 | async-start | bytes 8388608 | tf_op jit(solution)/shard_map/psum | solution.py:12
  834.5 2.0 copy-start.2
  912.2 3.4 copy-start
  917.7 181.3 %all-reduce.20.cloned.1.call-start = ((), (), s32[]{:S(2)}) async-start(), calls=%async_computation.4 | async-start | bytes 2097152 | tf_op jit(solution)/shard_map/psum | solution.py:124
  1021.6 4.8 copy-start.30
  1021.6 5.9 copy-start.29
  1036.7 361.5 %all-reduce.22.cloned.1.call-start = ((), (), s32[]{:S(2)}) async-start(), calls=%async_computation.5 | async-start | bytes 4194304 | tf_op jit(solution)/shard_map/psum | solution.py:12
  1041.3 1.9 copy-start.7
  1102.0 1.0 copy-start.25
  1248.5 6.6 copy-start.14
  1255.1 8.6 copy-start.11
  1320.7 10.0 copy-start.18
  1320.7 10.0 copy-start.19
  1320.7 10.0 copy-start.20
  1333.1 191.8 %all-reduce.28.cloned.1.call-start = ((), (), s32[]{:S(2)}) async-start(), calls=%async_computation.8 | async-start | bytes 8388608 | tf_op jit(solution)/shard_map/psum | solution.py:12
  1337.7 2.0 copy-start.3
  1415.4 3.4 copy-start.1
  1420.9 178.3 %all-reduce.24.cloned.1.call-start = ((), (), s32[]{:S(2)}) async-start(), calls=%async_computation.6 | async-start | bytes 2097152 | tf_op jit(solution)/shard_map/psum | solution.py:124
  1524.8 2.8 copy-start.32
  1524.8 2.9 copy-start.31
  1527.8 2.0 copy-start.8
  1537.0 361.7 %all-reduce.26.cloned.1.call-start = ((), (), s32[]{:S(2)}) async-start(), calls=%async_computation.7 | async-start | bytes 4194304 | tf_op jit(solution)/shard_map/psum | solution.py:12
  1541.6 1.9 copy-start.5
  1602.3 1.0 copy-start.26
  1748.8 6.6 copy-start.12
  1755.5 8.6 copy-start.9
  1821.0 10.2 copy-start.21
  1821.0 10.2 copy-start.22
  1821.0 10.2 copy-start.23
  1838.0 2.0 copy-start.4
Sparse Core Ops, SparseCore 0:
  407.5 110.7 all-reduce.31
  533.5 62.1 all-reduce.15
  829.9 64.9 all-reduce.17
  917.8 103.7 all-reduce.29
  1036.8 62.1 all-reduce.19
  1333.2 64.9 all-reduce.21
  1421.1 103.7 all-reduce.27
  1537.1 62.1 all-reduce.23
  1833.7 64.9 all-reduce.25
where the time goes:
time: 1950 us; the launch traced here: 1930 us
  waiting for transfers between devices  865 us (44%)
  other arithmetic  542 us (28%)
  local copies, waits for them, and re-layouts  358 us (18%)
  matrix products  129 us (7%)
  between operations  22.6 us (1%)
    psum x6, waiting for transfers between devices, from_root(): return lax.psum(jnp.where(mine, array, jnp.zeros_like(array)), axis)  446 us
    another operation x45, other arithmetic, local(): diag_factor = jnp.linalg.cholesky(diagonal_block)  239 us
    all_to_all x1, waiting for transfers between devices, local(): lax.all_to_all(col_buffer, 'col', split_axis=2, concat_axis=2, tiled=True)  205 us
    psum x3, waiting for transfers between devices, local(): diagonal_block = lax.psum(jnp.concatenate(blocks, axis=0), 'row')  154 us
    another operation x7, other arithmetic, local(): lax.linalg.triangular_solve(diag_factor, panel_strip, left_side=False, lo...  123 us
    broadcast_in_dim x36, local copies, waits for them, and re-layouts, local(): jnp.where((row_tiles == first_tile + offset)[:, None, None], factor_tiles...  104 us
    unnamed x95, local copies, waits for them, and re-layouts  74.2 us
    another operation x21, matrix products, local(): lax.linalg.triangular_solve(diag_factor, panel_strip, left_side=False, lo...  60.4 us
  transfers between devices with their start and end apart: 11, of which 11 were waited for; matrix products, arithmetic and copies ran while one was open for 6% of the time, Pallas kernels for 0%

commit v1 on v0

v1 whole, which is shorter than its diff:
```python
import functools
import jax
import jax.numpy as jnp
from jax import lax
from jax.experimental import pallas as pl
from jax.experimental.pallas import tpu as pltpu
from jax.sharding import PartitionSpec as P

T = 128
NB = 12
RHS = 256
WIDE = NB * T + RHS
HI = lax.Precision.HIGHEST
TDOT = (((0,), (0,)), ((), ()))


def split3(x):
    high = x.astype(jnp.bfloat16).astype(jnp.float32)
    rest = x - high
    mid = rest.astype(jnp.bfloat16).astype(jnp.float32)
    return high, mid, rest - mid


def inverse_factor(work, winv):
    sub = lax.broadcasted_iota(jnp.int32, (8, T), 0)
    lane = lax.broadcasted_iota(jnp.int32, (8, T), 1)
    for b in range(T // 8):
        rows = pl.ds(8 * b, 8)
        pa = work[rows, 0:T]
        pw = work[rows, T : 2 * T]
        cols = [jnp.broadcast_to(pa[:, 8 * b + j : 8 * b + j + 1], (8, T)) for j in range(8)]
        scale = jnp.zeros((8, T), jnp.float32)
        for j in range(8):
            pivot = jnp.broadcast_to(cols[j][j : j + 1, :], (8, T))
            root = lax.rsqrt(pivot)
            root = root * (1.5 - 0.5 * pivot * root * root)
            scale = jnp.where(sub == j, root, scale)
            if j == 7:
                break
            factor = jnp.where(sub > j, cols[j] * (root * root), 0.0)
            pa = pa - factor * jnp.broadcast_to(pa[j : j + 1, :], (8, T))
            pw = pw - factor * jnp.broadcast_to(pw[j : j + 1, :], (8, T))
            for m in range(j + 1, 8):
                cols[m] = cols[m] - factor * jnp.broadcast_to(cols[m][j : j + 1, :], (8, T))
        pw = pw * scale
        winv[rows, :] = pw
        if b < T // 8 - 1:
            pa = jnp.where(lane >= 8 * (b + 1), pa * scale, 0.0)
            left = split3(pa)
            right = split3(jnp.concatenate([pa, pw], axis=1))
            lhs = jnp.concatenate([left[0], left[0], left[1], left[1], left[0], left[2]], axis=0)
            rhs = jnp.concatenate([right[0], right[1], right[0], right[1], right[2], right[0]], axis=0)
            change = lax.dot_general(
                lhs.astype(jnp.bfloat16), rhs.astype(jnp.bfloat16), TDOT, preferred_element_type=jnp.float32
            )
            start = 8 * (b + 1)
            work[start:, :] = work[start:, :] - change[start:, :]


def factor_kernel(lead, rhs, out, mat, work, winv, acc):
    mat[...] = jnp.zeros_like(mat)
    for d in range(NB // 2 + 1):
        for i in range(d, NB):
            tile = lead[i - d, d] if d < 6 else lead[i, 6]
            mat[(i - d) * T : (i - d + 1) * T, i * T : (i + 1) * T] = tile.T if 0 < d < 6 else tile
    for d in range(7, NB):
        for i in range(d, NB):
            mat[(i - d) * T : (i - d + 1) * T, i * T : (i + 1) * T] = lead[i, NB - d]
    mat[:, NB * T :] = rhs[...]
    row_id = lax.broadcasted_iota(jnp.int32, (T, T), 0)
    col_id = lax.broadcasted_iota(jnp.int32, (T, T), 1)
    chunks = WIDE // 256

    @pl.loop(0, NB)
    def _(k):
        k0 = pl.multiple_of(k * T, T)
        kk = pl.ds(k0, T)

        @pl.loop(k // 2, chunks)
        def _(n):
            nn = pl.ds(pl.multiple_of(n * 256, 256), 256)
            acc[...] = mat[kk, nn]

            @pl.loop(0, (k + 3) // 4)
            def _(p):
                pp = pl.ds(pl.multiple_of(p * 512, 512), 512)
                left = mat[pp, kk]
                left = jnp.where(
                    lax.broadcasted_iota(jnp.int32, (512, T), 0) + p * 512 < k0, left, 0.0
                )
                acc[...] -= lax.dot_general(
                    left, mat[pp, nn], TDOT, precision=HI, preferred_element_type=jnp.float32
                )

            mat[kk, nn] = acc[...]

        work[:, 0:T] = mat[kk, kk]
        work[:, T : 2 * T] = jnp.where(row_id == col_id, 1.0, 0.0)
        inverse_factor(work, winv)

        @pl.loop(k // 2, chunks)
        def _(n):
            nn = pl.ds(pl.multiple_of(n * 256, 256), 256)
            mat[kk, nn] = jnp.dot(
                winv[...], mat[kk, nn], precision=HI, preferred_element_type=jnp.float32
            )

    out[...] = mat[:, NB * T :]


def factor(lead, rhs):
    return pl.pallas_call(
        factor_kernel,
        out_shape=jax.ShapeDtypeStruct((NB * T, RHS), jnp.float32),
        in_specs=[pl.BlockSpec(memory_space=pltpu.VMEM)] * 2,
        out_specs=pl.BlockSpec(memory_space=pltpu.VMEM),
        scratch_shapes=[
            pltpu.VMEM((NB * T, WIDE), jnp.float32),
            pltpu.VMEM((T, 2 * T), jnp.float32),
            pltpu.VMEM((T, T), jnp.float32),
            pltpu.VMEM((T, 256), jnp.float32),
        ],
        compiler_params=pltpu.CompilerParams(vmem_limit_bytes=56 * 1024 * 1024),
        cost_estimate=pl.CostEstimate(flops=150_000_000_000, bytes_accessed=10_000_000, transcendentals=0),
    )(lead, rhs)


def gather_tiles(tiles, *index):
    return tiles.at[index].get(mode="promise_in_bounds")


def local(front, children, child_maps, fill):
    n_row = lax.axis_size("row")
    n_col = lax.axis_size("col")
    half = n_row // 2
    r = lax.axis_index("row")
    c = lax.axis_index("col")
    h = r // half
    lane = r % half
    tiles = children[0, :, :, 0].transpose(2, 0, 1, 3)
    groups, child_rows = tiles.shape[:2]
    own = front[0, :, :, 0]
    parent_rows, _, parent_cols, _ = own.shape
    per = n_col // half

    heads = child_maps[:, ::n_col]
    shifts = heads % n_col
    blocks = heads // n_col
    wanted = jnp.arange(n_col)
    by_shift = jnp.argmax(shifts[:, None, :] == wanted[None, :, None], axis=2)
    hits = blocks[:, None, :] == jnp.arange(parent_cols)[None, :, None]
    by_block = jnp.argmax(hits, axis=2)
    has_block = jnp.any(hits, axis=2)
    first = by_block[:, 0]

    fill_rows = lax.dynamic_index_in_dim(fill.reshape(parent_rows, n_row, parent_cols, n_col), r, 1, keepdims=False)
    fill_local = lax.dynamic_index_in_dim(fill_rows, c, 2, keepdims=False).astype(jnp.float32)
    base = own * fill_local[:, None, :, None]

    send_group = by_shift[h][(wanted - c) % n_col]
    lead_rows = lax.dynamic_slice_in_dim(tiles, per * first[h], per, axis=1)
    lead_got = lax.all_to_all(lead_rows[send_group], "col", 0, 0, tiled=True)
    rest_got = lax.all_to_all(tiles[send_group], "col", 0, 0, tiled=True)

    own_blocks = by_block[h]
    source = (c - shifts[h][own_blocks]) % n_col
    lead_blocks = jnp.where(has_block[h][:, None, None, None], lead_got[source], 0)
    strip = lax.all_to_all(lead_blocks, "row", 0, 0, tiled=True).reshape(n_row, per, T, T)
    lead_front = base[:2].transpose(2, 0, 1, 3)
    strip_front = lax.all_to_all(lead_front, "row", 0, 0, tiled=True)
    lead_gather = lax.all_gather(lead_blocks[0], "row", axis=0)
    front_gather = lax.all_gather(lead_front[0], "row", axis=0)

    def lead_column(parts, fronts):
        total = fronts.transpose(1, 0, 2, 3).reshape(n_col, T, T)
        for child in range(2):
            places = (wanted - shifts[child, first[child]]) % n_col
            total += parts[child * half + places % half, places // half].astype(jnp.float32)
        return total

    mine = lead_column(strip, strip_front)[:NB].reshape(NB * T, T)
    corner = lead_column(lead_gather, front_gather)[:NB]
    corner = corner[(c + jnp.arange(NB // 2 + 1)) % NB]
    lead = lax.all_gather(corner, "col", axis=0)
    pairs = [(i * n_col + j, (j % n_row) * n_col + 2 * i + j // n_row) for i in range(n_row) for j in range(n_col)]
    moved = lax.ppermute(mine, ("row", "col"), pairs)
    solved = factor(lead, jnp.concatenate([mine, moved], axis=1))

    exponent = jnp.floor(jnp.log2(jnp.maximum(jnp.max(jnp.abs(solved), axis=0), 1e-30))) + 1.0
    coded = jnp.clip(jnp.round(solved * jnp.exp2(15.0 - exponent)), -32767.0, 32767.0).astype(jnp.int16)
    tagged = jnp.concatenate([coded, jnp.broadcast_to(exponent.astype(jnp.int16), (16, 2 * T))], axis=0)
    right = lax.all_gather(tagged[:, :T], "row", axis=0)
    left = lax.all_gather(tagged[:, T:].T, "col", axis=0)
    left = left.reshape(parent_rows * T, NB * T + 16)
    left_rows = left[:, : NB * T].astype(jnp.float32) * jnp.exp2(left[:, NB * T :][:, :1].astype(jnp.float32) - 15.0)
    right_cols = right[:, : NB * T].astype(jnp.float32) * jnp.exp2(right[:, NB * T :][:, :1].astype(jnp.float32) - 15.0)
    right_cols = right_cols.transpose(1, 0, 2).reshape(NB * T, parent_cols * T)
    update = jnp.dot(left_rows, right_cols, precision=lax.Precision.HIGH, preferred_element_type=jnp.float32)
    update = update.reshape(parent_rows, T, parent_cols, T)

    tile_of = c * n_row + r
    panel = solved[:, T:].reshape(NB, T, T)
    steps = jnp.arange(NB)
    upper = jnp.arange(T)[:, None] <= jnp.arange(T)[None, :]
    keep = (steps < tile_of)[:, None, None] | ((steps == tile_of)[:, None, None] & upper[None])
    panel = jnp.where(keep, panel, 0.0).transpose(0, 2, 1)
    panel = jnp.concatenate([panel, jnp.zeros((n_col - NB, T, T), jnp.float32)], axis=0)
    panel = lax.all_to_all(panel, "col", 0, 0, tiled=True)

    ranks = jnp.sum(
        (shifts[:, None, :] % half == shifts[:, :, None] % half)
        & (jnp.arange(groups)[None, None, :] < jnp.arange(groups)[None, :, None]),
        axis=2,
    )
    rows = jnp.arange(n_row)
    lanes = (lane + shifts[h][None, :]) % half == (rows % half)[:, None]
    slots = jnp.argmax(lanes[:, None, :] & (ranks[h][None, None, :] == jnp.arange(2)[None, :, None]), axis=2)
    turn = (rows[:, None, None] + n_row * jnp.arange(2)[None, None, :] - lane - shifts[h][slots][:, :, None]) % n_col
    send_rows = (per * slots[:, :, None] + turn // half).reshape(n_row, 4)
    send_from = (c - shifts[h]) % n_col
    row_send = rest_got[send_from[None, None, :], send_rows[:, :, None]]
    got = lax.all_to_all(row_send, "row", 0, 0, tiled=True)

    parent = base
    local_rows = jnp.arange(parent_rows)
    for child in range(2):
        group = by_block[child][local_rows // 2]
        place = (r + n_row * (local_rows % 2) - shifts[child][group]) % n_col
        row_slot = 2 * ranks[child][group] + local_rows % 2
        part = got[
            (child * half + place % half)[:, None], row_slot[:, None], by_block[child][None, :]
        ]
        valid = has_block[child][local_rows // 2][:, None] & has_block[child][None, :]
        part = jnp.where(valid[:, :, None, None], part, 0).transpose(0, 2, 1, 3)
        parent = parent + part.astype(jnp.float32)

    result = parent - update
    row_tiles = r + n_row * local_rows
    col_tiles = c + n_col * jnp.arange(parent_cols)
    cleared = (row_tiles < NB)[:, None] & (col_tiles >= NB)[None, :]
    result = jnp.where(cleared[:, None, :, None], 0.0, result)
    result = result.at[:, :, 0].set(jnp.where(c < NB, panel, result[:, :, 0]))
    return result[None, :, :, None]


def solution(mesh):
    placed = (
        P("row", None, None, "col", None, None),
        P("row", None, None, "col", None, None),
        P(),
        P(),
    )
    return jax.shard_map(
        local,
        mesh=mesh,
        in_specs=placed,
        out_specs=P("row", None, None, "col", None, None),
        check_vma=False,
    )
```

time: 1950 us -> 736 us (0.38)
  waiting for transfers between devices: 865 us -> 311 us
  other arithmetic: 542 us -> 31.1 us
  local copies, waits for them, and re-layouts: 358 us -> 106 us
  Pallas kernels: 0 us -> 136 us
  matrix products: 129 us -> 26.8 us
  blocking collectives: 0 us -> 65.2 us
  starting transfers between devices: 15.5 us -> 38.4 us
    psum x9 -> x0, waiting for transfers between devices: 600 us -> none  [the longest x6 446 us: from_root(): return lax.psum(jnp.where(mine, array, jnp.zeros_like(array)), axis)]
    another operation x60 -> x3, other arithmetic: 374 us -> 1.91 us  [the longest x1 0.68 us: local(): by_block = jnp.argmax(hits, axis=2)]
    pallas_call x0 -> x1, Pallas kernels: none -> 136 us  [factor(): pl.pallas_call(factor_kernel, out_shape=jax.ShapeDtypeStruct((NB * T, RHS...]
    broadcast_in_dim x39 -> x3, local copies, waits for them, and re-layouts: 104 us -> 0.1 us  [the longest x1 0.08 us: local(): shifts[h][slots][:, :, None]]
    select_n x26 -> x11, other arithmetic: 78 us -> 1.22 us  [the longest x1 1.12 us: local(): jnp.where(has_block[h][:, None, None, None], lead_got[source], 0)]
    another operation x39 -> x0, matrix products: 76.8 us -> none  [the longest x21 60.4 us: local(): lax.linalg.triangular_solve(diag_factor, panel_strip, left_side=False, lo...]
    all_gather x0 -> x2, blocking collectives: none -> 65.2 us  [the longest x1 45.5 us: local(): left = lax.all_gather(tagged[:, T:].T, 'col', axis=0)]
    unnamed x95 -> x27, local copies, waits for them, and re-layouts: 74.2 us -> 13.6 us
  transfers between devices with their start and end apart: 11 -> 10, of which waited for: 11 -> 7; matrix products, arithmetic and copies ran while one was open for 6% -> 14% of each run, Pallas kernels for 0% -> 0%
where the time goes in v1:
time: 736 us; the launch traced here: 734 us
  waiting for transfers between devices  311 us (42%)
  Pallas kernels  136 us (18%)
  local copies, waits for them, and re-layouts  106 us (14%)
  blocking collectives  65.2 us (9%)
  starting transfers between devices  38.4 us (5%)
  other arithmetic  31.1 us (4%)
  matrix products  26.8 us (4%)
  between operations  19.6 us (3%)
    all_to_all x1, waiting for transfers between devices, local(): rest_got = lax.all_to_all(tiles[send_group], 'col', 0, 0, tiled=True)  158 us
    pallas_call x1, Pallas kernels, factor(): pl.pallas_call(factor_kernel, out_shape=jax.ShapeDtypeStruct((NB * T, RHS...  136 us
    all_to_all x1, waiting for transfers between devices, local(): got = lax.all_to_all(row_send, 'row', 0, 0, tiled=True)  86.9 us
    all_gather x1, blocking collectives, local(): left = lax.all_gather(tagged[:, T:].T, 'col', axis=0)  45.5 us
    dot_general x1, matrix products, local(): jnp.dot(left_rows, right_cols, precision=lax.Precision.HIGH, preferred_el...  26.8 us
    all_gather x1, waiting for transfers between devices, local(): front_gather = lax.all_gather(lead_front[0], 'row', axis=0)  21.2 us
    all_to_all x1, waiting for transfers between devices, local(): lead_got = lax.all_to_all(lead_rows[send_group], 'col', 0, 0, tiled=True)  20.7 us
    all_gather x1, blocking collectives, local(): right = lax.all_gather(tagged[:, :T], 'row', axis=0)  19.7 us
  transfers between devices with their start and end apart: 10, of which 7 were waited for; matrix products, arithmetic and copies ran while one was open for 14% of the time, Pallas kernels for 0%

profile of v1, /device:TPU:0, one launch (start us, length us, event | category | flops | bytes accessed | tf_op | source)
XLA Modules:
  0.0 734.2 jit_solution(9442285033914430978)
XLA Ops:
  6.5 1.0 reshape.1016
  7.9 5.5 bitcast_multiply_fusion
  13.4 3.4 copy-done.1
  16.9 1.1 copy.82
  18.0 4.6 all-to-all-start.3
  22.8 0.7 iota_reduce_fusion
  27.5 1.2 dynamic-slice_bitcast_fusion
  28.7 2.2 gather_fusion.14
  30.9 7.6 %all-to-all-done.3 = f32[8,2,128,128]{3,2,1,0:T(8,128)S(1)} async-done(((f32[8,2,128,128]{3,2,1,0:T(8,128)}), f32[8,2,128,128]{3,2,1,0:T(8,128)S(1)}, u32[]{:S(2)}, u32[]{:S(2)}) %all-to-all-start.3) | async-done | bytes 1048608 | tf_op jit(solution)/shard_map/all_to_all | solution.py:170
  38.5 7.9 %all-to-all-start.2 = ((bf16[16,4,128,128]{3,2,1,0:T(8,128)(2,1)}), bf16[16,4,128,128]{3,2,1,0:T(8,128)(2,1)}, u32[]{:S(2)}, u32[]{:S(2)}) async-start(bf16[16,4,128,128]{3,2,1,0:T(8,128)(2,1)} %gather_fusion.14), calls=%async_computation.2 | async-start | bytes 4194304 | tf_op jit(solution)/shard_map/all_to_all | solution.py:162
  46.4 8.5 %gather_fusion.2 = bf16[16,24,128,128]{3,2,1,0:T(8,128)(2,1)} fusion(bf16[6,24,128,128]{3,2,0,1:T(8,128)(2,1)} %bitcast.149, s32[1024]{0:T(1024)S(1)} %pad_clamp_fusion.6), kind=kCustom, calls=%fused_computation.2 | custom fusion | bytes 25165888 | tf_op jit(solution)/shard_map/gather | solution.py:163
  55.8 20.7 %all-to-all-done.2 = bf16[16,4,128,128]{3,2,1,0:T(8,128)(2,1)} async-done(((bf16[16,4,128,128]{3,2,1,0:T(8,128)(2,1)}), bf16[16,4,128,128]{3,2,1,0:T(8,128)(2,1)}, u32[]{:S(2)}, u32[]{:S(2)}) %all-to-all-start.2) | async-done | bytes 2097184 | tf_op jit(solution)/shard_map/all_to_all | solution.py:162
  76.5 4.9 all-to-all-start
  81.5 2.3 gather_fusion.16
  83.8 1.1 broadcast_select_fusion
  84.9 1.6 slice.187
  86.6 0.7 slice.186
  92.5 1.3 fusion.75
  93.8 15.8 %all-gather.11.cloned.1.call-done = bf16[8,4,128,128]{3,2,1,0:T(8,128)(2,1)} async-done(((bf16[1,4,128,128]{3,2,1,0:T(8,128)(2,1)}), bf16[8,4,128,128]{3,2,1,0:T(8,128)(2,1)}) %all-gather.11.cloned.1.call-update) | async-done | bytes 1048592 | tf_op jit(solution)/shard_map/all_gather | solution.py:171
  109.6 1.9 gather_fusion.18
  111.5 1.9 gather_fusion.17
  113.4 21.2 %all-gather.9.cloned.1.call-done = f32[8,2,128,128]{3,2,0,1:T(8,128)} async-done(((f32[1,2,128,128]{3,2,0,1:T(8,128)}), f32[8,2,128,128]{3,2,0,1:T(8,128)}) %all-gather.9.cloned.1.call-update) | async-done | bytes 1048592 | tf_op jit(solution)/shard_map/all_gather | solution.py:172
  134.6 1.3 fusion.13
  135.9 1.3 gather_fusion.19
  138.8 158.0 %all-to-all-done = bf16[16,24,128,128]{3,2,1,0:T(8,128)(2,1)} async-done(((bf16[16,24,128,128]{3,2,1,0:T(8,128)(2,1)}), bf16[16,24,128,128]{3,2,1,0:T(8,128)(2,1)}, u32[]{:S(2)}, u32[]{:S(2)}) %all-to-all-start) | async-done | bytes 12582944 | tf_op jit(solution)/shard_map/all_to_all | solution.py:163
  296.8 10.0 %all-to-all-start.4 = ((bf16[8,4,128,128]{3,2,1,0:T(8,128)(2,1)}), bf16[8,4,128,128]{3,2,1,0:T(8,128)(2,1)S(1)}, u32[]{:S(2)}, u32[]{:S(2)}) async-start(bf16[8,4,128,128]{3,2,1,0:T(8,128)(2,1)} %broadcast_select_fusion), calls=%async_computation.4 | async-start | bytes 2097152 | tf_op jit(solution)/shard_map/all_to_all | solution.py:168
  308.0 14.0 %gather_fusion.4 = bf16[192,128,128]{2,1,0:T(8,128)(2,1)} fusion(bf16[16,24,128,128]{3,2,1,0:T(8,128)(2,1)} %all-to-all-done, s32[192]{0:T(256)S(1)} %reshape.1056), kind=kCustom, calls=%fused_computation.4 | custom fusion | bytes 12584448 | tf_op jit(solution)/shard_map/gather | solution.py:221
  322.1 0.7 all-to-all-done.4
  322.8 4.9 all-to-all-start.1
  327.7 0.7 gather_fusion.10
  328.4 0.7 gather_fusion.12
  329.0 0.7 gather_fusion.11
  329.7 0.7 gather_fusion.5
  330.4 0.7 gather_fusion.7
  331.0 0.7 gather_fusion.6
  332.6 1.4 gather_fusion.21
  334.0 1.4 gather_fusion.20
  335.5 1.2 fusion.12
  336.7 0.9 collective-permute-start
  337.8 0.7 gather_fusion.9
  338.5 0.7 gather_fusion
  340.4 0.7 broadcast_and_fusion.1
  341.0 0.7 broadcast_and_fusion.2
  341.7 1.2 pad_maximum_fusion.rhs
  343.0 86.9 %all-to-all-done.1 = bf16[8,4,6,128,128]{4,3,2,1,0:T(8,128)(2,1)} async-done(((bf16[8,4,6,128,128]{4,3,2,1,0:T(8,128)(2,1)}), bf16[8,4,6,128,128]{4,3,2,1,0:T(8,128)(2,1)}, u32[]{:S(2)}, u32[]{:S(2)}) %all-to-all-start.1) | async-done | bytes 6291488 | tf_op jit(solution)/shard_map/all_to_all | solution.py:222
  429.9 6.0 gather_fusion.13
  435.8 6.0 gather_fusion.8
  441.9 136.2 %shard_map.46 = f32[1536,256]{1,0:T(8,128)} custom-call(f32[16,7,128,128]{3,2,1,0:T(8,128)} %bitcast.167, f32[1536,256]{1,0:T(8,128)} %pad_maximum_fusion.rhs), custom_call_target="tpu_custom_call" | custom-call | flops 149999992832 | bytes 10000000 | tf_op jit(solution)/shard_map/pallas_call | solution.py:112
  578.1 1.5 abs_reduce_fusion
  579.6 1.6 clamp_convert_fusion
  581.3 19.7 %all-gather.15 = s16[12416,128]{1,0:T(8,128)(2,1)S(1)} all-gather(s16[1552,128]{1,0:T(8,128)(2,1)S(1)} %get-tuple-element.30), channel_id=4, replica_groups=mesh['row'=8,'col'=16] {'row'}, dimensions={0}, use_global_device_ids=true | all-gather | bytes 3575808 | tf_op jit(solution)/shard_map/all_gather | solution.py:192
  601.2 1.0 slice.200
  602.2 45.5 %all-gather.14 = s16[2048,1552]{0,1:T(8,128)(2,1)S(1)} all-gather(s16[128,1552]{0,1:T(8,128)(2,1)S(1)} %get-tuple-element.31), channel_id=3, replica_groups=mesh['row'=8,'col'=16] {'col'}, dimensions={0}, use_global_device_ids=true | all-gather | bytes 6754304 | tf_op jit(solution)/shard_map/all_gather | solution.py:193
  647.8 6.8 convert_multiply_fusion
  654.6 12.6 %copy.91 = f32[2048,1536]{1,0:T(8,128)} copy(f32[2048,1536]{0,1:T(8,128)} %convert_multiply_fusion) | data formatting | bytes 25165824 | tf_op jit(solution)/shard_map/dot_general | solution.py:198
  667.2 3.4 copy.97
  670.6 1.4 copy.87
  672.2 1.1 concatenate.35
  673.3 5.1 all-to-all-start.5
  678.5 26.8 %fusion.1 = f32[16,128,8,128]{3,1,2,0:T(8,128)S(1)} fusion(f32[16,128,8,128]{3,1,2,0:T(8,128)} %copy-done.1, bf16[16,8,128,128]{3,2,1,0:T(8,128)(2,1)} %bitcast.155, bf16[16,8,128,128]{3,2,1,0:T(8,128)(2,1)} %bitcast.156, pred[16,8]{1,0:T(8,128)(4,1)S(1)} %copy-done.6, pred[16,8]{1,0:T(8,128)(4,1)S(1)} %copy-done.7, pred[16,8]{1,0:T(8,128)(4,1)S(1)} %copy-done.8, ...), kind=kOutput, calls=%fused_computation.25 | convolution fusion | flops 19347275776 | bytes 40898944 | tf_op jit(solution)/shard_map/dot_general | solution.py:198
  705.3 3.4 copy-done
  708.7 3.2 copy.101
  711.9 2.4 fusion.11
  714.3 13.3 %copy.89 = f32[1,16,128,1,8,128]{5,4,3,2,1,0:T(8,128)} copy(f32[1,16,128,1,8,128]{5,2,4,1,3,0:T(8,128)} %fusion.11) | data formatting | bytes 16777216 | tf_op jit(solution)/shard_map/scatter | solution.py:242
  (110 shorter events, 10.4 us)
Async XLA Ops:
  13.4 3.4 copy-start.1
  16.8 5.7 copy-start.9
  18.0 20.5 %all-to-all-start.3 = ((f32[8,2,128,128]{3,2,1,0:T(8,128)}), f32[8,2,128,128]{3,2,1,0:T(8,128)S(1)}, u32[]{:S(2)}, u32[]{:S(2)}) async-start(f32[8,2,128,128]{3,2,1,0:T(8,128)} %copy.82), calls=%async_computation.3 | async-start | bytes 2097152 | tf_op jit(solution)/shard_map/all_to_all | solution.py:170
  38.5 16.5 %copy-start.3 = (f32[8,2,128,128]{3,2,1,0:T(8,128)}, f32[8,2,128,128]{3,2,1,0:T(8,128)S(1)}, u32[]{:S(2)}) copy-start(f32[8,2,128,128]{3,2,1,0:T(8,128)S(1)} %all-to-all-done.3) | copy-start | bytes 3145732
  38.5 38.0 %all-to-all-start.2 = ((bf16[16,4,128,128]{3,2,1,0:T(8,128)(2,1)}), bf16[16,4,128,128]{3,2,1,0:T(8,128)(2,1)}, u32[]{:S(2)}, u32[]{:S(2)}) async-start(bf16[16,4,128,128]{3,2,1,0:T(8,128)(2,1)} %gather_fusion.14), calls=%async_computation.2 | async-start | bytes 4194304 | tf_op jit(solution)/shard_map/all_to_all | solution.py:162
  76.5 220.3 %all-to-all-start = ((bf16[16,24,128,128]{3,2,1,0:T(8,128)(2,1)}), bf16[16,24,128,128]{3,2,1,0:T(8,128)(2,1)}, u32[]{:S(2)}, u32[]{:S(2)}) async-start(bf16[16,24,128,128]{3,2,1,0:T(8,128)(2,1)} %gather_fusion.2), calls=%async_computation | async-start | bytes 25165824 | tf_op jit(solution)/shard_map/all_to_all | solution.py:163
  81.4 28.2 %all-gather.11.cloned.1.call-start = ((), (), s32[]{:S(2)}) async-start(), calls=%async_computation.7 | async-start | bytes 1179648 | tf_op jit(solution)/shard_map/all_gather | solution.py:171
  86.5 48.1 %all-gather.9.cloned.1.call-start = ((), (), s32[]{:S(2)}) async-start(), calls=%async_computation.6 | async-start | bytes 1179648 | tf_op jit(solution)/shard_map/all_gather | solution.py:172
  87.3 354.6 %all-gather.13.cloned.1.call-start = ((), (), s32[]{:S(2)}) async-start(), calls=%async_computation.8 | async-start | bytes 7798784 | tf_op jit(solution)/shard_map/all_gather | solution.py:184
  296.8 26.0 %all-to-all-start.4 = ((bf16[8,4,128,128]{3,2,1,0:T(8,128)(2,1)}), bf16[8,4,128,128]{3,2,1,0:T(8,128)(2,1)S(1)}, u32[]{:S(2)}, u32[]{:S(2)}) async-start(bf16[8,4,128,128]{3,2,1,0:T(8,128)(2,1)} %broadcast_select_fusion), calls=%async_computation.4 | async-start | bytes 2097152 | tf_op jit(solution)/shard_map/all_to_all | solution.py:168
  322.8 9.7 %copy-start.4 = (f32[8,2,128,128]{3,2,1,0:T(8,128)S(1)}, f32[8,2,128,128]{3,2,1,0:T(8,128)}, u32[]{:S(2)}) copy-start(f32[8,2,128,128]{3,2,1,0:T(8,128)} %copy-done.3) | copy-start | bytes 3145732
  322.8 107.1 %all-to-all-start.1 = ((bf16[8,4,6,128,128]{4,3,2,1,0:T(8,128)(2,1)}), bf16[8,4,6,128,128]{4,3,2,1,0:T(8,128)(2,1)}, u32[]{:S(2)}, u32[]{:S(2)}) async-start(bf16[8,4,6,128,128]{4,3,2,1,0:T(8,128)(2,1)} %bitcast.150), calls=%async_computation.1 | async-start | bytes 12582912 | tf_op jit(solution)/shard_map/all_to_all | solution.py:222
  336.7 5.0 collective-permute-start
  581.2 20.0 %copy-start.2 = (f32[1536,256]{1,0:T(8,128)S(1)}, f32[1536,256]{1,0:T(8,128)}, u32[]{:S(2)}) copy-start(f32[1536,256]{1,0:T(8,128)} %shard_map.46) | copy-start | bytes 4718596
  667.1 4.9 copy-start.5
  667.1 4.9 copy-start.10
  667.1 4.9 copy-start.11
  667.1 11.3 %copy-start.6 = (pred[16,8]{1,0:T(8,128)(4,1)S(1)}, pred[16,8]{1,0:T(8,128)(4,1)}, u32[]{:S(2)}) copy-start(pred[16,8]{1,0:T(8,128)(4,1)} %broadcast_and_fusion) | copy-start | bytes 388
  667.1 11.3 %copy-start.7 = (pred[16,8]{1,0:T(8,128)(4,1)S(1)}, pred[16,8]{1,0:T(8,128)(4,1)}, u32[]{:S(2)}) copy-start(pred[16,8]{1,0:T(8,128)(4,1)} %broadcast_and_fusion.1) | copy-start | bytes 388
  667.2 11.3 %copy-start.8 = (pred[16,8]{1,0:T(8,128)(4,1)S(1)}, pred[16,8]{1,0:T(8,128)(4,1)}, u32[]{:S(2)}) copy-start(pred[16,8]{1,0:T(8,128)(4,1)} %broadcast_and_fusion.2) | copy-start | bytes 388
  673.3 38.6 %all-to-all-start.5 = ((f32[16,128,128]{2,1,0:T(8,128)}), f32[16,128,128]{2,1,0:T(8,128)S(1)}, u32[]{:S(2)}, u32[]{:S(2)}) async-start(f32[16,128,128]{2,1,0:T(8,128)} %concatenate.35), calls=%async_computation.5 | async-start | bytes 2097152 | tf_op jit(solution)/shard_map/all_to_all | solution.py:208
  705.3 3.4 copy-start
Sparse Core Ops, SparseCore 0:
  86.7 22.9 all-gather.10
  111.3 23.2 all-gather.8
  137.4 170.1 all-gather.12

commit v2 on v1

--- a/solution.py
+++ b/solution.py
@@ -57,7 +57,60 @@
             work[start:, :] = work[start:, :] - change[start:, :]
 
 
-def factor_kernel(lead, rhs, out, mat, work, winv, acc):
+MESH = pl.DeviceIdType.MESH
+Q = 4
+PART = T // Q
+GROUPS = 6
+ROWS = 24
+CODED = NB * T
+LEFT = CODED + T
+RIGHT = CODED + 16
+
+
+def exchange_factor_kernel(
+    pick, turn, slots, lead, rhs, out, got,
+    mat, work, winv, acc, packed, own_sem, col_send, col_recv, row_send, row_recv, *recv,
+):
+    n_row, n_col = lax.axis_size("row"), lax.axis_size("col")
+    r, c = lax.axis_index("row"), lax.axis_index("col")
+    barrier = pltpu.get_barrier_semaphore()
+    for d in range(1, n_col):
+        pl.semaphore_signal(barrier, inc=1, device_id={"col": lax.rem(c + d, n_col)}, device_id_type=MESH)
+    for e in range(1, n_row):
+        pl.semaphore_signal(barrier, inc=1, device_id={"row": lax.rem(r + e, n_row)}, device_id_type=MESH)
+    pl.semaphore_wait(barrier, n_col + n_row - 2)
+
+    def col_copy(q, d):
+        return pltpu.make_async_remote_copy(
+            src_ref=slots.at[q, d],
+            dst_ref=recv[q].at[d],
+            send_sem=col_send.at[q, d],
+            recv_sem=col_recv.at[q, d],
+            device_id={"col": lax.rem(c + d, n_col)},
+            device_id_type=MESH,
+        )
+
+    def col_own(q):
+        return pltpu.make_async_copy(slots.at[q, 0], recv[q].at[0], own_sem.at[q])
+
+    def row_copy(q, e):
+        return pltpu.make_async_remote_copy(
+            src_ref=packed.at[q, e],
+            dst_ref=got.at[q, e],
+            send_sem=row_send.at[q, e],
+            recv_sem=row_recv.at[q, e],
+            device_id={"row": lax.rem(r + e, n_row)},
+            device_id_type=MESH,
+        )
+
+    def row_own(q):
+        return pltpu.make_async_copy(packed.at[q, 0], got.at[q, 0], own_sem.at[Q + q])
+
+    for q in range(Q):
+        col_own(q).start()
+        for d in range(1, n_col):
+            col_copy(q, d).start()
+
     mat[...] = jnp.zeros_like(mat)
     for d in range(NB // 2 + 1):
         for i in range(d, NB):
@@ -105,24 +158,299 @@
                 winv[...], mat[kk, nn], precision=HI, preferred_element_type=jnp.float32
             )
 
+        for q in range(Q):
+
+            @pl.when(k == (q + 1) * (NB // Q) - 1)
+            def _(q=q):
+                col_own(q).wait()
+                for d in range(1, n_col):
+                    col_copy(q, d).wait_recv()
+
+                @pl.loop(0, n_row * 4)
+                def _(i):
+                    for g in range(GROUPS):
+                        packed[q, i // 4, i % 4, g] = recv[q][pick[g], turn[i]]
+
+                row_own(q).start()
+                for e in range(1, n_row):
+                    row_copy(q, e).start()
+
     out[...] = mat[:, NB * T :]
 
-
-def factor(lead, rhs):
+    for q in range(Q):
+        row_own(q).wait()
+        for d in range(1, n_col):
+            col_copy(q, d).wait_send()
+        for e in range(1, n_row):
+            row_copy(q, e).wait()
+
+
+def exchange_factor(pick, turn, slots, lead, rhs):
+    n_row, n_col = lax.axis_size("row"), lax.axis_size("col")
+    vmem = pl.BlockSpec(memory_space=pltpu.VMEM)
+    smem = pl.BlockSpec(memory_space=pltpu.SMEM)
+    hbm = pl.BlockSpec(memory_space=pl.ANY)
+    dma = pltpu.SemaphoreType.DMA
     return pl.pallas_call(
-        factor_kernel,
-        out_shape=jax.ShapeDtypeStruct((NB * T, RHS), jnp.float32),
-        in_specs=[pl.BlockSpec(memory_space=pltpu.VMEM)] * 2,
-        out_specs=pl.BlockSpec(memory_space=pltpu.VMEM),
+        exchange_factor_kernel,
+        out_shape=(
+            jax.ShapeDtypeStruct((NB * T, RHS), jnp.float32),
+            jax.ShapeDtypeStruct((Q, n_row, 4, GROUPS, PART, T), jnp.bfloat16),
+        ),
+        in_specs=[smem, smem, hbm, vmem, vmem],
+        out_specs=(vmem, hbm),
         scratch_shapes=[
             pltpu.VMEM((NB * T, WIDE), jnp.float32),
             pltpu.VMEM((T, 2 * T), jnp.float32),
             pltpu.VMEM((T, T), jnp.float32),
             pltpu.VMEM((T, 256), jnp.float32),
+            pltpu.VMEM((Q, n_row, 4, GROUPS, PART, T), jnp.bfloat16),
+            dma((2 * Q,)),
+            dma((Q, n_col)),
+            dma((Q, n_col)),
+            dma((Q, n_row)),
+            dma((Q, n_row)),
+        ]
+        + [pltpu.VMEM((n_col, ROWS, PART, T), jnp.bfloat16)] * Q,
+        compiler_params=pltpu.CompilerParams(
+            vmem_limit_bytes=60 * 1024 * 1024, collective_id=0, has_side_effects=True
+        ),
+    )(pick, turn, slots, lead, rhs)
+
+
+def update_kernel(
+    fill, row_pick, col_pick, left, right, got, front, out,
+    lbuf, rbuf, rhi, rlo, lhi, llo, acc, lsend, lrecv, rsend, rrecv,
+):
+    r, c = lax.axis_index("row"), lax.axis_index("col")
+    x, z = c // 4, c % 4
+    y, core = r // 2, r % 2
+    step = 1 - 2 * core
+
+    def at_col(dx, dz):
+        return lax.rem(x + dx + 4, 4) * 4 + lax.rem(z + dz + 4, 4)
+
+    def at_row(dy, flip):
+        return lax.rem(y + dy, 4) * 2 + (1 - core if flip else core)
+
+    barrier = pltpu.get_barrier_semaphore()
+    for d in (1, -1):
+        pl.semaphore_signal(barrier, inc=1, device_id={"col": at_col(d, 0)}, device_id_type=MESH)
+        pl.semaphore_signal(barrier, inc=1, device_id={"col": at_col(0, d)}, device_id_type=MESH)
+    for dy, flip in ((1, False), (2, False), (3, False), (0, True)):
+        pl.semaphore_signal(barrier, inc=1, device_id={"row": at_row(dy, flip)}, device_id_type=MESH)
+    pl.semaphore_wait(barrier, 8)
+
+    lbuf[c] = left[...]
+    rbuf[r] = right[...]
+    sent = []
+
+    def send_left(block, part, target):
+        copy = pltpu.make_async_remote_copy(
+            src_ref=lbuf.at[block, pl.ds(part * 64, 64)],
+            dst_ref=lbuf.at[block, pl.ds(part * 64, 64)],
+            send_sem=lsend.at[len(sent)],
+            recv_sem=lrecv.at[block, part],
+            device_id={"col": target},
+            device_id_type=MESH,
+        )
+        copy.start()
+        sent.append(copy)
+
+    def wait_left(block, part):
+        pltpu.make_async_remote_copy(
+            src_ref=lbuf.at[block, pl.ds(part * 64, 64)],
+            dst_ref=lbuf.at[block, pl.ds(part * 64, 64)],
+            send_sem=lsend.at[0],
+            recv_sem=lrecv.at[block, part],
+            device_id={"col": at_col(1, 0)},
+            device_id_type=MESH,
+        ).wait_recv()
+
+    rsent = []
+
+    def send_right(block, target):
+        copy = pltpu.make_async_remote_copy(
+            src_ref=rbuf.at[block],
+            dst_ref=rbuf.at[block],
+            send_sem=rsend.at[len(rsent)],
+            recv_sem=rrecv.at[block],
+            device_id={"row": target},
+            device_id_type=MESH,
+        )
+        copy.start()
+        rsent.append(copy)
+
+    def wait_right(block):
+        pltpu.make_async_remote_copy(
+            src_ref=rbuf.at[block],
+            dst_ref=rbuf.at[block],
+            send_sem=rsend.at[0],
+            recv_sem=rrecv.at[block],
+            device_id={"row": at_row(0, True)},
+            device_id_type=MESH,
+        ).wait_recv()
+
+    def place(part, along, across):
+        return at_col(across, along) if part == 0 else at_col(along, across)
+
+    def assemble(first, last):
+        @pl.loop(first * 8, last * 8)
+        def _(i):
+            li, lj = i // 8, i % 8
+            for q in range(Q):
+                where = pl.ds((li * T + q * PART) * 8 + lj, PART, stride=8)
+                value = front[where, :] * fill[i]
+                for child in range(2):
+                    entry = got[q, row_pick[child, li], row_pick[2 + child, li], col_pick[child, lj]]
+                    valid = row_pick[4 + child, li] * col_pick[2 + child, lj]
+                    value = value + jnp.where(valid > 0, entry.astype(jnp.float32), 0.0)
+                out[where, :] = value
+
+    for part in range(2):
+        send_left(c, part, place(part, 1, 0))
+        send_left(c, part, place(part, -1, 0))
+    send_right(r, at_row(0, True))
+    for dy in (1, 3, 2):
+        send_right(r, at_row(dy, False))
+    for part in range(2):
+        send_left(c, part, place(part, 0, 1))
+        send_left(c, part, place(part, 0, -1))
+    assemble(0, 4)
+    for part in range(2):
+        block = place(part, -step, 0)
+        wait_left(block, part)
+        send_left(block, part, place(part, step, 0))
+        send_left(block, part, place(part, 0, 1))
+        send_left(block, part, place(part, 0, -1))
+    for part in range(2):
+        block = place(part, step, 0)
+        wait_left(block, part)
+        send_left(block, part, place(part, 0, 1))
+        send_left(block, part, place(part, 0, -1))
+    for dy in (1, 3):
+        wait_right(at_row(dy, False))
+        send_right(at_row(dy, False), at_row(0, True))
+    assemble(4, 8)
+    for part in range(2):
+        block = place(part, 2, 0)
+        wait_left(block, part)
+        send_left(block, part, place(part, 0, 1))
+        send_left(block, part, place(part, 0, -1))
+    for along in (0, -step, step):
+        for part in range(2):
+            block = place(part, along, -step)
+            wait_left(block, part)
+            send_left(block, part, place(part, 0, step))
+    wait_right(at_row(2, False))
+    send_right(at_row(2, False), at_row(0, True))
+    assemble(8, 12)
+    for part in range(2):
+        block = place(part, 2, -step)
+        wait_left(block, part)
+        send_left(block, part, place(part, 0, step))
+    assemble(12, 16)
+    for dy in range(4):
+        wait_right(at_row(dy, True))
+    for along in range(4):
+        for across in (step, 2):
+            for part in range(2):
+                wait_left(place(part, along, across), part)
+
+    def split(coded, scale):
+        value = coded.astype(jnp.int32).astype(jnp.float32) * scale
+        high = value.astype(jnp.bfloat16)
+        return value, high, (value - high.astype(jnp.float32)).astype(jnp.bfloat16)
+
+    @pl.loop(0, 8)
+    def _(j):
+        scale = jnp.exp2(rbuf[j, CODED:RIGHT, :].astype(jnp.int32).astype(jnp.float32)[0:1, :] - 15.0)
+        lanes = pl.ds(pl.multiple_of((j % 2) * T, T), T)
+
+        @pl.loop(0, NB)
+        def _(k):
+            rows = pl.ds(pl.multiple_of(k * T, T), T)
+            _, high, low = split(rbuf[j, rows, :], scale)
+            rhi[j // 2, rows, lanes] = high
+            rlo[j // 2, rows, lanes] = low
+
+    row_id = lax.broadcasted_iota(jnp.int32, (T, T), 0)
+    col_id = lax.broadcasted_iota(jnp.int32, (T, T), 1)
+    in_panel = c < NB
+    panel_lanes = pl.ds(pl.multiple_of(jnp.minimum(c, NB - 1) * T, T), T)
+
+    @pl.loop(0, 4)
+    def _(s):
+        @pl.loop(0, 4)
+        def _(m):
+            li = s * 4 + m
+            rows = pl.ds(pl.multiple_of(m * T, T), T)
+            scale = jnp.exp2(lbuf[li, :, CODED:LEFT].astype(jnp.int32).astype(jnp.float32) - 15.0)
+
+            @pl.loop(0, NB)
+            def _(k):
+                lanes = pl.ds(pl.multiple_of(k * T, T), T)
+                _, high, low = split(lbuf[li, :, lanes], scale)
+                lhi[rows, lanes] = high
+                llo[rows, lanes] = low
+
+        @pl.loop(0, 4)
+        def _(n):
+            total = jnp.dot(lhi[...], rlo[n], preferred_element_type=jnp.float32)
+            total += jnp.dot(llo[...], rhi[n], preferred_element_type=jnp.float32)
+            total += jnp.dot(lhi[...], rhi[n], preferred_element_type=jnp.float32)
+            acc[...] = total
+
+            @pl.loop(0, 8)
+            def _(i):
+                m, j = i // 2, i % 2
+                li, lj = s * 4 + m, n * 2 + j
+                row_tile, col_tile = r + 8 * li, c + 16 * lj
+                where = pl.ds(li * T * 8 + lj, T, stride=8)
+                change = acc[pl.ds(pl.multiple_of(m * T, T), T), pl.ds(pl.multiple_of(j * T, T), T)]
+                cleared = (row_tile < NB) & (col_tile >= NB)
+                out[where, :] = jnp.where(cleared, 0.0, out[where, :] - change)
+
+    @pl.when(in_panel)
+    def _():
+        @pl.loop(0, 16)
+        def _(li):
+            row_tile = r + 8 * li
+            scale = jnp.exp2(lbuf[li, :, CODED:LEFT].astype(jnp.int32).astype(jnp.float32) - 15.0)
+            value = lbuf[li, :, panel_lanes].astype(jnp.int32).astype(jnp.float32) * scale
+            keep = (row_tile > c) | ((row_tile == c) & (row_id >= col_id))
+            out[pl.ds(li * T * 8, T, stride=8), :] = jnp.where(keep, value, 0.0)
+
+    for copy in sent + rsent:
+        copy.wait_send()
+
+
+def update(fill, row_pick, col_pick, left, right, got, front):
+    vmem = pl.BlockSpec(memory_space=pltpu.VMEM)
+    smem = pl.BlockSpec(memory_space=pltpu.SMEM)
+    dma = pltpu.SemaphoreType.DMA
+    return pl.pallas_call(
+        update_kernel,
+        out_shape=jax.ShapeDtypeStruct(front.shape, jnp.float32),
+        in_specs=[smem] * 3 + [vmem] * 4,
+        out_specs=vmem,
+        scratch_shapes=[
+            pltpu.VMEM((16, T, LEFT), jnp.int16),
+            pltpu.VMEM((8, RIGHT, T), jnp.int16),
+            pltpu.VMEM((4, CODED, 256), jnp.bfloat16),
+            pltpu.VMEM((4, CODED, 256), jnp.bfloat16),
+            pltpu.VMEM((4 * T, CODED), jnp.bfloat16),
+            pltpu.VMEM((4 * T, CODED), jnp.bfloat16),
+            pltpu.VMEM((4 * T, 256), jnp.float32),
+            dma((32,)),
+            dma((16, 2)),
+            dma((8,)),
+            dma((8,)),
         ],
-        compiler_params=pltpu.CompilerParams(vmem_limit_bytes=56 * 1024 * 1024),
-        cost_estimate=pl.CostEstimate(flops=150_000_000_000, bytes_accessed=10_000_000, transcendentals=0),
-    )(lead, rhs)
+        compiler_params=pltpu.CompilerParams(
+            vmem_limit_bytes=60 * 1024 * 1024, collective_id=1, has_side_effects=True
+        ),
+    )(fill, row_pick, col_pick, left, right, got, front)
 
 
 def gather_tiles(tiles, *index):
@@ -155,18 +483,19 @@
 
     fill_rows = lax.dynamic_index_in_dim(fill.reshape(parent_rows, n_row, parent_cols, n_col), r, 1, keepdims=False)
     fill_local = lax.dynamic_index_in_dim(fill_rows, c, 2, keepdims=False).astype(jnp.float32)
-    base = own * fill_local[:, None, :, None]
-
+    base = own[:2] * fill_local[:2, None, :, None]
+
+    lead_rows = lax.dynamic_slice_in_dim(tiles, per * first[h], per, axis=1)
     send_group = by_shift[h][(wanted - c) % n_col]
-    lead_rows = lax.dynamic_slice_in_dim(tiles, per * first[h], per, axis=1)
     lead_got = lax.all_to_all(lead_rows[send_group], "col", 0, 0, tiled=True)
-    rest_got = lax.all_to_all(tiles[send_group], "col", 0, 0, tiled=True)
+    parts = tiles.reshape(groups, child_rows, Q, PART, T).transpose(2, 0, 1, 3, 4)
+    slots = parts[:, by_shift[h]]
 
     own_blocks = by_block[h]
     source = (c - shifts[h][own_blocks]) % n_col
     lead_blocks = jnp.where(has_block[h][:, None, None, None], lead_got[source], 0)
     strip = lax.all_to_all(lead_blocks, "row", 0, 0, tiled=True).reshape(n_row, per, T, T)
-    lead_front = base[:2].transpose(2, 0, 1, 3)
+    lead_front = base.transpose(2, 0, 1, 3)
     strip_front = lax.all_to_all(lead_front, "row", 0, 0, tiled=True)
     lead_gather = lax.all_gather(lead_blocks[0], "row", axis=0)
     front_gather = lax.all_gather(lead_front[0], "row", axis=0)
@@ -184,63 +513,44 @@
     lead = lax.all_gather(corner, "col", axis=0)
     pairs = [(i * n_col + j, (j % n_row) * n_col + 2 * i + j // n_row) for i in range(n_row) for j in range(n_col)]
     moved = lax.ppermute(mine, ("row", "col"), pairs)
-    solved = factor(lead, jnp.concatenate([mine, moved], axis=1))
-
-    exponent = jnp.floor(jnp.log2(jnp.maximum(jnp.max(jnp.abs(solved), axis=0), 1e-30))) + 1.0
-    coded = jnp.clip(jnp.round(solved * jnp.exp2(15.0 - exponent)), -32767.0, 32767.0).astype(jnp.int16)
-    tagged = jnp.concatenate([coded, jnp.broadcast_to(exponent.astype(jnp.int16), (16, 2 * T))], axis=0)
-    right = lax.all_gather(tagged[:, :T], "row", axis=0)
-    left = lax.all_gather(tagged[:, T:].T, "col", axis=0)
-    left = left.reshape(parent_rows * T, NB * T + 16)
-    left_rows = left[:, : NB * T].astype(jnp.float32) * jnp.exp2(left[:, NB * T :][:, :1].astype(jnp.float32) - 15.0)
-    right_cols = right[:, : NB * T].astype(jnp.float32) * jnp.exp2(right[:, NB * T :][:, :1].astype(jnp.float32) - 15.0)
-    right_cols = right_cols.transpose(1, 0, 2).reshape(NB * T, parent_cols * T)
-    update = jnp.dot(left_rows, right_cols, precision=lax.Precision.HIGH, preferred_element_type=jnp.float32)
-    update = update.reshape(parent_rows, T, parent_cols, T)
-
-    tile_of = c * n_row + r
-    panel = solved[:, T:].reshape(NB, T, T)
-    steps = jnp.arange(NB)
-    upper = jnp.arange(T)[:, None] <= jnp.arange(T)[None, :]
-    keep = (steps < tile_of)[:, None, None] | ((steps == tile_of)[:, None, None] & upper[None])
-    panel = jnp.where(keep, panel, 0.0).transpose(0, 2, 1)
-    panel = jnp.concatenate([panel, jnp.zeros((n_col - NB, T, T), jnp.float32)], axis=0)
-    panel = lax.all_to_all(panel, "col", 0, 0, tiled=True)
-
     ranks = jnp.sum(
         (shifts[:, None, :] % half == shifts[:, :, None] % half)
         & (jnp.arange(groups)[None, None, :] < jnp.arange(groups)[None, :, None]),
         axis=2,
     )
-    rows = jnp.arange(n_row)
+    rows = (r + jnp.arange(n_row)) % n_row
     lanes = (lane + shifts[h][None, :]) % half == (rows % half)[:, None]
-    slots = jnp.argmax(lanes[:, None, :] & (ranks[h][None, None, :] == jnp.arange(2)[None, :, None]), axis=2)
-    turn = (rows[:, None, None] + n_row * jnp.arange(2)[None, None, :] - lane - shifts[h][slots][:, :, None]) % n_col
-    send_rows = (per * slots[:, :, None] + turn // half).reshape(n_row, 4)
-    send_from = (c - shifts[h]) % n_col
-    row_send = rest_got[send_from[None, None, :], send_rows[:, :, None]]
-    got = lax.all_to_all(row_send, "row", 0, 0, tiled=True)
-
-    parent = base
+    choice = jnp.argmax(lanes[:, None, :] & (ranks[h][None, None, :] == jnp.arange(2)[None, :, None]), axis=2)
+    turn = (rows[:, None, None] + n_row * jnp.arange(2)[None, None, :] - lane - shifts[h][choice][:, :, None]) % n_col
+    turn = (per * choice[:, :, None] + turn // half).reshape(4 * n_row)
+    solved, got = exchange_factor(
+        shifts[h].astype(jnp.int32),
+        turn.astype(jnp.int32),
+        slots,
+        lead,
+        jnp.concatenate([mine, moved], axis=1),
+    )
+
+    exponent = jnp.floor(jnp.log2(jnp.maximum(jnp.max(jnp.abs(solved), axis=0), 1e-30))) + 1.0
+    coded = jnp.clip(jnp.round(solved * jnp.exp2(15.0 - exponent)), -32767.0, 32767.0).astype(jnp.int16)
+    tag = exponent.astype(jnp.int16)
+    right = jnp.concatenate([coded[:, :T], jnp.broadcast_to(tag[:T], (16, T))], axis=0)
+    left = jnp.concatenate([coded[:, T:].T, jnp.broadcast_to(tag[T:, None], (T, T))], axis=1)
+
     local_rows = jnp.arange(parent_rows)
+    row_pick, row_slot, row_valid = [], [], []
     for child in range(2):
         group = by_block[child][local_rows // 2]
         place = (r + n_row * (local_rows % 2) - shifts[child][group]) % n_col
-        row_slot = 2 * ranks[child][group] + local_rows % 2
-        part = got[
-            (child * half + place % half)[:, None], row_slot[:, None], by_block[child][None, :]
-        ]
-        valid = has_block[child][local_rows // 2][:, None] & has_block[child][None, :]
-        part = jnp.where(valid[:, :, None, None], part, 0).transpose(0, 2, 1, 3)
-        parent = parent + part.astype(jnp.float32)
-
-    result = parent - update
-    row_tiles = r + n_row * local_rows
-    col_tiles = c + n_col * jnp.arange(parent_cols)
-    cleared = (row_tiles < NB)[:, None] & (col_tiles >= NB)[None, :]
-    result = jnp.where(cleared[:, None, :, None], 0.0, result)
-    result = result.at[:, :, 0].set(jnp.where(c < NB, panel, result[:, :, 0]))
-    return result[None, :, :, None]
+        row_pick.append((r - child * half - place % half) % n_row)
+        row_slot.append(2 * ranks[child][group] + local_rows % 2)
+        row_valid.append(has_block[child][local_rows // 2])
+    row_pick = jnp.stack(row_pick + row_slot + row_valid).astype(jnp.int32)
+    col_pick = jnp.concatenate([by_block, has_block.astype(by_block.dtype)]).astype(jnp.int32)
+    result = update(
+        fill_local.reshape(-1), row_pick, col_pick, left, right, got, own.reshape(-1, T)
+    )
+    return result.reshape(front.shape)
 
 
 def solution(mesh):

time: 736 us -> 537 us (0.73)
  waiting for transfers between devices: 311 us -> 110 us
  Pallas kernels: 136 us -> 311 us
  blocking collectives: 65.2 us -> 0 us
  local copies, waits for them, and re-layouts: 106 us -> 62.9 us
  matrix products: 26.8 us -> 0 us
  starting transfers between devices: 38.4 us -> 16.1 us
  other arithmetic: 31.1 us -> 13.5 us
    all_to_all x3 -> x0, waiting for transfers between devices: 245 us -> none  [the longest x1 158 us: local(): rest_got = lax.all_to_all(tiles[send_group], 'col', 0, 0, tiled=True)]
    pallas_call x1 -> x2, Pallas kernels: 136 us -> 311 us  [the longest x1 215 us: exchange_factor(): pl.pallas_call(exchange_factor_kernel, out_shape=(jax.ShapeDtypeStruct((N...]
    all_gather x2 -> x0, blocking collectives: 65.2 us -> none  [the longest x1 45.5 us: local(): left = lax.all_gather(tagged[:, T:].T, 'col', axis=0)]
    dot_general x1 -> x0, matrix products: 26.8 us -> none  [local(): jnp.dot(left_rows, right_cols, precision=lax.Precision.HIGH, preferred_el...]
    all_gather x1, waiting for transfers between devices: 0.01 us -> 18.8 us  [local(): lead = lax.all_gather(corner, 'col', axis=0)]
    all_to_all x3 -> x0, starting transfers between devices: 14.9 us -> none  [the longest x1 5.1 us: local(): panel = lax.all_to_all(panel, 'col', 0, 0, tiled=True)]
    gather x11 -> x8, local copies, waits for them, and re-layouts: 38 us -> 23.8 us  [the longest x2 20.4 us: local(): slots = parts[:, by_shift[h]]]
    scatter x1 -> x0, local copies, waits for them, and re-layouts: 13.3 us -> none  [local(): result = result.at[:, :, 0].set(jnp.where(c < NB, panel, result[:, :, 0]))]
  transfers between devices with their start and end apart: 10 -> 7, of which waited for: 7 -> 6; matrix products, arithmetic and copies ran while one was open for 14% -> 10% of each run, Pallas kernels for 0% -> 0%
where the time goes in v2:
time: 537 us; the launch traced here: 533 us
  Pallas kernels  311 us (58%)
  waiting for transfers between devices  110 us (20%)
  local copies, waits for them, and re-layouts  62.9 us (12%)
  between operations  19 us (4%)
  starting transfers between devices  16.1 us (3%)
  other arithmetic  13.5 us (3%)
    pallas_call x1, Pallas kernels, exchange_factor(): pl.pallas_call(exchange_factor_kernel, out_shape=(jax.ShapeDtypeStruct((N...  215 us
    pallas_call x1, Pallas kernels, update(): pl.pallas_call(update_kernel, out_shape=jax.ShapeDtypeStruct(front.shape,...  95.5 us
    all_to_all x1, waiting for transfers between devices, local(): lead_got = lax.all_to_all(lead_rows[send_group], 'col', 0, 0, tiled=True)  29.6 us
    all_gather x1, waiting for transfers between devices, local(): front_gather = lax.all_gather(lead_front[0], 'row', axis=0)  21.2 us
    gather x2, local copies, waits for them, and re-layouts, local(): slots = parts[:, by_shift[h]]  20.4 us
    all_gather x1, waiting for transfers between devices, local(): lead = lax.all_gather(corner, 'col', axis=0)  18.8 us
    all_gather x1, waiting for transfers between devices, local(): lead_gather = lax.all_gather(lead_blocks[0], 'row', axis=0)  14.2 us
    all_to_all x1, waiting for transfers between devices, local(): lax.all_to_all(lead_blocks, 'row', 0, 0, tiled=True)  13.5 us
  transfers between devices with their start and end apart: 7, of which 6 were waited for; matrix products, arithmetic and copies ran while one was open for 10% of the time, Pallas kernels for 0%

profile of v2, /device:TPU:0, one launch (start us, length us, event | category | flops | bytes accessed | tf_op | source)
XLA Modules:
  0.0 532.6 jit_solution(11009953875366217558)
XLA Ops:
  6.5 0.8 slice.78
  7.6 0.5 iota_reduce_fusion
  8.2 0.6 compare_reduce_fusion
  8.8 0.5 fusion.53
  10.7 0.7 gather_fusion.10
  12.0 1.2 dynamic-slice_bitcast_fusion
  13.2 2.1 gather_fusion.11
  15.3 8.0 %all-to-all-start = ((bf16[16,4,128,128]{3,2,1,0:T(8,128)(2,1)}), bf16[16,4,128,128]{3,2,1,0:T(8,128)(2,1)S(1)}, u32[]{:S(2)}, u32[]{:S(2)}) async-start(bf16[16,4,128,128]{3,2,1,0:T(8,128)(2,1)} %gather_fusion.11), calls=%async_computation | async-start | bytes 4194304 | tf_op jit(solution)/shard_map/all_to_all | solution.py:490
  23.4 0.6 gather_fusion.12
  24.1 29.6 %all-to-all-done = bf16[16,4,128,128]{3,2,1,0:T(8,128)(2,1)S(1)} async-done(((bf16[16,4,128,128]{3,2,1,0:T(8,128)(2,1)}), bf16[16,4,128,128]{3,2,1,0:T(8,128)(2,1)S(1)}, u32[]{:S(2)}, u32[]{:S(2)}) %all-to-all-start) | async-done | bytes 2097184 | tf_op jit(solution)/shard_map/all_to_all | solution.py:490
  53.7 0.7 gather_fusion.13
  54.4 1.1 broadcast_select_fusion
  55.6 1.6 slice.142
  57.3 0.2 reshape.1030
  57.6 0.2 copy.58
  57.8 0.3 fusion.1
  58.0 0.7 slice.141
  58.8 0.5 fusion.51
  62.9 0.6 constant_dynamic-slice_fusion
  63.5 1.2 fusion.42
  64.7 14.2 %all-gather.7.cloned.1.call-done = bf16[8,4,128,128]{3,2,1,0:T(8,128)(2,1)} async-done(((bf16[1,4,128,128]{3,2,1,0:T(8,128)(2,1)}), bf16[8,4,128,128]{3,2,1,0:T(8,128)(2,1)}) %all-gather.7.cloned.1.call-update) | async-done | bytes 1048592 | tf_op jit(solution)/shard_map/all_gather | solution.py:500
  78.9 1.9 gather_fusion.15
  80.8 1.9 gather_fusion.14
  82.7 21.2 %all-gather.5.cloned.1.call-done = f32[8,2,128,128]{3,2,0,1:T(8,128)} async-done(((f32[1,2,128,128]{3,2,0,1:T(8,128)}), f32[8,2,128,128]{3,2,0,1:T(8,128)}) %all-gather.5.cloned.1.call-update) | async-done | bytes 1048592 | tf_op jit(solution)/shard_map/all_gather | solution.py:501
  103.8 1.3 fusion.3
  105.1 1.4 gather_fusion.16
  106.5 1.1 copy.53
  107.5 3.6 all-to-all-start.1
  111.1 0.7 gather_fusion.2
  111.8 0.7 gather_fusion
  112.6 0.3 fusion.4
  112.8 0.2 dynamic-slice_reduce_fusion
  113.2 0.7 and_reduce_fusion
  114.1 12.9 %all-to-all-done.1 = f32[8,2,128,128]{3,2,1,0:T(8,128)S(1)} async-done(((f32[8,2,128,128]{3,2,1,0:T(8,128)}), f32[8,2,128,128]{3,2,1,0:T(8,128)S(1)}, u32[]{:S(2)}, u32[]{:S(2)}) %all-to-all-start.1) | async-done | bytes 1048608 | tf_op jit(solution)/shard_map/all_to_all | solution.py:499
  127.0 3.6 all-to-all-start.2
  130.6 0.7 gather_fusion.8
  131.3 0.7 gather_fusion.5
  132.0 0.7 gather_fusion.4
  132.9 13.5 %all-to-all-done.2 = bf16[8,4,128,128]{3,2,1,0:T(8,128)(2,1)S(1)} async-done(((bf16[8,4,128,128]{3,2,1,0:T(8,128)(2,1)}), bf16[8,4,128,128]{3,2,1,0:T(8,128)(2,1)S(1)}, u32[]{:S(2)}, u32[]{:S(2)}) %all-to-all-start.2) | async-done | bytes 1048608 | tf_op jit(solution)/shard_map/all_to_all | solution.py:497
  146.4 1.4 gather_fusion.18
  147.9 1.4 gather_fusion.17
  149.3 1.3 fusion.2
  150.6 0.9 collective-permute-start
  151.5 0.7 convert_element_type.61.fill
  152.1 0.7 gather_fusion.3
  152.8 0.7 gather_fusion.1
  153.5 0.7 gather_fusion.7
  154.1 0.7 gather_fusion.6
  155.2 6.0 %copy.68 = bf16[6,24,4,32,128]{4,3,1,0,2:T(8,128)(2,1)} copy(bf16[6,24,4,32,128]{4,3,2,0,1:T(8,128)(2,1)} %bitcast.127) | data formatting | bytes 9437184 | tf_op jit(solution)/shard_map/reshape | solution.py:491
  161.2 8.7 %gather_fusion.9 = bf16[16,4,24,32,128]{4,3,2,1,0:T(8,128)(2,1)} fusion(bf16[4,6,24,32,128]{4,3,2,1,0:T(8,128)(2,1)} %bitcast.122, s32[1024]{0:T(1024)S(1)} %pad_clamp_fusion.5), kind=kCustom, calls=%fused_computation.9 | custom fusion | bytes 25165888 | tf_op jit(solution)/shard_map/gather | solution.py:492
  169.9 11.6 %copy.67 = bf16[16,4,24,32,128]{4,3,2,0,1:T(8,128)(2,1)} copy(bf16[16,4,24,32,128]{4,3,2,1,0:T(8,128)(2,1)} %gather_fusion.9) | data formatting | bytes 25165824 | tf_op jit(solution)/shard_map/gather | solution.py:492
  181.6 0.6 stack.2.row_pick
  182.2 0.6 pad_add_fusion.2.col_pick
  182.8 0.5 fusion.43.turn
  183.3 1.2 pad_maximum_fusion.rhs
  184.6 18.8 %all-gather.9.cloned.1.call-done = f32[112,128,128]{2,1,0:T(8,128)} async-done(((f32[7,128,128]{2,1,0:T(8,128)}), f32[112,128,128]{2,1,0:T(8,128)}) %all-gather.9.cloned.1.call-update) | async-done | bytes 7340048 | tf_op jit(solution)/shard_map/all_gather | solution.py:513
  203.4 215.5 %shard_map.46 = (f32[1536,256]{1,0:T(8,128)}, bf16[4,8,4,6,32,128]{5,4,3,2,1,0:T(8,128)(2,1)}) custom-call(s32[6]{0:T(128)} %copy-done, s32[32]{0:T(128)} %fusion.43.turn, bf16[4,16,24,32,128]{4,3,2,1,0:T(8,128)(2,1)} %bitcast.123, f32[16,7,128,128]{3,2,1,0:T(8,128)} %bitcast.126, f32[1536,256]{1,0:T(8,128)} %pad_maximum_fusion.rhs), custom_call_target="tpu_custom_call" | custom-call | tf_op jit(solution)/shard_map/pallas_call | solution.py:194
  418.9 1.6 abs_reduce_fusion
  420.5 0.2 copy-done.1
  420.7 0.2 clamp_convert_fusion
  421.0 1.1 copy.55.left
  422.1 0.8 pad_add_fusion.1.right
  422.9 95.5 %shard_map.47 = f32[16384,128]{1,0:T(8,128)} custom-call(f32[128]{0:T(128)} %convert_element_type.61.fill, s32[6,16]{1,0:T(8,128)} %stack.2.row_pick, s32[4,8]{1,0:T(4,128)} %pad_add_fusion.2.col_pick, s16[128,1664]{1,0:T(8,128)(2,1)} %copy.55.left, s16[1552,128]{1,0:T(8,128)(2,1)} %pad_add_fusion.1.right, ...), custom_call_target="tpu_custom_call" | custom-call | tf_op jit(solution)/shard_map/pallas_call | solution.py:432
  518.5 7.6 %copy.70 = f32[1,16,128,1,8,128]{5,4,3,2,1,0:T(8,128)} copy(f32[1,16,128,1,8,128]{5,4,3,2,1,0:T(8,128)} %bitcast.124) | data formatting | bytes 16777216
  (70 shorter events, 2.1 us)
Async XLA Ops:
  15.3 38.3 %all-to-all-start = ((bf16[16,4,128,128]{3,2,1,0:T(8,128)(2,1)}), bf16[16,4,128,128]{3,2,1,0:T(8,128)(2,1)S(1)}, u32[]{:S(2)}, u32[]{:S(2)}) async-start(bf16[16,4,128,128]{3,2,1,0:T(8,128)(2,1)} %gather_fusion.11), calls=%async_computation | async-start | bytes 4194304 | tf_op jit(solution)/shard_map/all_to_all | solution.py:490
  23.3 55.6 %all-gather.7.cloned.1.call-start = ((), (), s32[]{:S(2)}) async-start(), calls=%async_computation.4 | async-start | bytes 1179648 | tf_op jit(solution)/shard_map/all_gather | solution.py:500
  23.4 107.2 %copy-start = (s32[6]{0:T(128)}, s32[6]{0:T(128)S(1)}, u32[]{:S(2)}) copy-start(s32[6]{0:T(128)S(1)} %get-tuple-element.31.pick) | copy-start | bytes 76
  24.1 33.2 %copy-start.2 = (s32[128,128]{1,0:T(8,128)S(1)}, s32[128,128]{1,0:T(8,128)}, u32[]{:S(2)}) copy-start(s32[128,128]{1,0:T(8,128)} %param.7) | copy-start | bytes 196612
  55.6 2.2 slice-start
  57.2 46.6 %all-gather.5.cloned.1.call-start = ((), (), s32[]{:S(2)}) async-start(), calls=%async_computation.3 | async-start | bytes 1179648 | tf_op jit(solution)/shard_map/all_gather | solution.py:501
  58.7 144.7 %all-gather.9.cloned.1.call-start = ((), (), s32[]{:S(2)}) async-start(), calls=%async_computation.5 | async-start | bytes 7798784 | tf_op jit(solution)/shard_map/all_gather | solution.py:513
  107.5 19.4 %all-to-all-start.1 = ((f32[8,2,128,128]{3,2,1,0:T(8,128)}), f32[8,2,128,128]{3,2,1,0:T(8,128)S(1)}, u32[]{:S(2)}, u32[]{:S(2)}) async-start(f32[8,2,128,128]{3,2,1,0:T(8,128)} %copy.53), calls=%async_computation.1 | async-start | bytes 2097152 | tf_op jit(solution)/shard_map/all_to_all | solution.py:499
  127.0 19.5 %all-to-all-start.2 = ((bf16[8,4,128,128]{3,2,1,0:T(8,128)(2,1)}), bf16[8,4,128,128]{3,2,1,0:T(8,128)(2,1)S(1)}, u32[]{:S(2)}, u32[]{:S(2)}) async-start(bf16[8,4,128,128]{3,2,1,0:T(8,128)(2,1)} %broadcast_select_fusion), calls=%async_computation.2 | async-start | bytes 2097152 | tf_op jit(solution)/shard_map/all_to_all | solution.py:497
  150.6 32.8 %collective-permute-start = (f32[1536,128]{1,0:T(8,128)S(1)}, f32[1536,128]{1,0:T(8,128)S(1)}, u32[]{:S(2)}, u32[]{:S(2)}) collective-permute-start(f32[1536,128]{1,0:T(8,128)S(1)} %bitcast.129), channel_id=1, source_target_pairs={{0,0},{1,16},{2,32},{3,48},{4,64},{5,80},{6,96},{7,112},{8,1},{9,1... | collective-permute-start | bytes 2359304 | tf_op jit(solution)/shard_map/ppermute | solution.py:515
  418.9 1.9 copy-start.1
Sparse Core Ops, SparseCore 0:
  57.3 21.5 all-gather.6
  80.6 23.1 all-gather.4
  106.6 96.7 all-gather.8

commit v3 on v2

--- a/solution.py
+++ b/solution.py
@@ -61,65 +61,256 @@
 Q = 4
 PART = T // Q
 GROUPS = 6
-ROWS = 24
+REST = 20
+LEAD_ROWS = 4
+CORNER = NB // 2 + 1
 CODED = NB * T
 LEFT = CODED + T
 RIGHT = CODED + 16
+X_START = (0, 2, 4, 6)
+ROW_START = (3, 6, 8, 11)
 
 
 def exchange_factor_kernel(
-    pick, turn, slots, lead, rhs, out, got,
-    mat, work, winv, acc, packed, own_sem, col_send, col_recv, row_send, row_recv, *recv,
+    pick, turn, pair, src_row, src_tile, valid, lead_slots, slots, lead_front, out, got,
+    mat, work, winv, acc, packed, lead_recv, strip_send, strip, corner_strip, strip_front, corner_front,
+    mine, moved, corner, own_sem, lead_send, lead_got, front_send, front_got, strip_sent, strip_got,
+    move_sem, ring_send, ring_got, twin_send, twin_got, z_send, z_got, x_send, x_got, row_send, row_got, *buffers,
 ):
     n_row, n_col = lax.axis_size("row"), lax.axis_size("col")
+    z_recv, x_out, x_recv = buffers[:Q], buffers[Q : 2 * Q], buffers[2 * Q :]
     r, c = lax.axis_index("row"), lax.axis_index("col")
+    x, z = c // 4, c % 4
+    core = r % 2
+    step = 1 - 2 * core
+    twin = r + step
+
+    def at_col(dx, dz):
+        return lax.rem(x + dx + 4, 4) * 4 + lax.rem(z + dz + 4, 4)
+
+    def row_peer(e):
+        return lax.rem(r + e, n_row)
+
+    def remote(src, dst, sent, landed, device):
+        return pltpu.make_async_remote_copy(
+            src_ref=src, dst_ref=dst, send_sem=sent, recv_sem=landed, device_id=device, device_id_type=MESH
+        )
+
+    target_row, target_col = c % n_row, 2 * r + c // n_row
+    origin_row, origin_col = c // 2, lax.rem(n_row * c + r, n_col)
+    moves = (target_row != r) | (target_col != c)
+
     barrier = pltpu.get_barrier_semaphore()
     for d in range(1, n_col):
         pl.semaphore_signal(barrier, inc=1, device_id={"col": lax.rem(c + d, n_col)}, device_id_type=MESH)
     for e in range(1, n_row):
-        pl.semaphore_signal(barrier, inc=1, device_id={"row": lax.rem(r + e, n_row)}, device_id_type=MESH)
-    pl.semaphore_wait(barrier, n_col + n_row - 2)
-
-    def col_copy(q, d):
-        return pltpu.make_async_remote_copy(
-            src_ref=slots.at[q, d],
-            dst_ref=recv[q].at[d],
-            send_sem=col_send.at[q, d],
-            recv_sem=col_recv.at[q, d],
-            device_id={"col": lax.rem(c + d, n_col)},
-            device_id_type=MESH,
-        )
-
-    def col_own(q):
-        return pltpu.make_async_copy(slots.at[q, 0], recv[q].at[0], own_sem.at[q])
+        pl.semaphore_signal(barrier, inc=1, device_id={"row": row_peer(e)}, device_id_type=MESH)
+
+    @pl.when(moves)
+    def _():
+        pl.semaphore_signal(
+            barrier, inc=1, device_id={"row": origin_row, "col": origin_col}, device_id_type=MESH
+        )
+
+    pl.semaphore_wait(barrier, n_col + n_row - 2 + jnp.where(moves, 1, 0))
+
+    def lead_copy(d):
+        return remote(
+            lead_slots.at[d], lead_recv.at[d], lead_send.at[d], lead_got.at[d], {"col": lax.rem(c + d, n_col)}
+        )
+
+    def front_copy(e, whole):
+        if whole:
+            return remote(
+                lead_front.at[0], corner_front.at[r], front_send.at[1, e], front_got.at[1, r], {"row": row_peer(e)}
+            )
+        return remote(
+            lead_front.at[row_peer(e)], strip_front.at[r], front_send.at[0, e], front_got.at[0, r], {"row": row_peer(e)}
+        )
+
+    def strip_copy(e, whole):
+        if whole:
+            return remote(
+                strip_send.at[0], corner_strip.at[r], strip_sent.at[1, e], strip_got.at[1, r], {"row": row_peer(e)}
+            )
+        return remote(
+            strip_send.at[row_peer(e)], strip.at[r], strip_sent.at[0, e], strip_got.at[0, r], {"row": row_peer(e)}
+        )
+
+    lead_own = pltpu.make_async_copy(lead_slots.at[0], lead_recv.at[0], own_sem.at[0])
+    lead_own.start()
+    for d in range(1, n_col):
+        lead_copy(d).start()
+    for e in range(1, n_row):
+        for whole in (False, True):
+            front_copy(e, whole).start()
+    strip_front[r] = lead_front[r]
+    corner_front[r] = lead_front[0]
+
+    def z_copy(q, d):
+        return remote(
+            slots.at[q, d], z_recv[q].at[d], z_send.at[q, d], z_got.at[q, d], {"col": at_col(0, d)}
+        )
+
+    def z_own(q):
+        return pltpu.make_async_copy(slots.at[q, 0], z_recv[q].at[0], own_sem.at[1 + q])
+
+    def x_copy(q, d):
+        return remote(
+            x_out[q].at[d], x_recv[q].at[d], x_send.at[q, d], x_got.at[q, d], {"col": at_col(d, 0)}
+        )
 
     def row_copy(q, e):
-        return pltpu.make_async_remote_copy(
-            src_ref=packed.at[q, e],
-            dst_ref=got.at[q, e],
-            send_sem=row_send.at[q, e],
-            recv_sem=row_recv.at[q, e],
-            device_id={"row": lax.rem(r + e, n_row)},
-            device_id_type=MESH,
+        return remote(
+            packed.at[q, e], got.at[q, e], row_send.at[q, e], row_got.at[q, e], {"row": row_peer(e)}
         )
 
     def row_own(q):
-        return pltpu.make_async_copy(packed.at[q, 0], got.at[q, 0], own_sem.at[Q + q])
-
-    for q in range(Q):
-        col_own(q).start()
-        for d in range(1, n_col):
-            col_copy(q, d).start()
-
+        return pltpu.make_async_copy(packed.at[q, 0], got.at[q, 0], own_sem.at[1 + Q + q])
+
+    def z_start(q):
+        z_own(q).start()
+        for d in range(1, 4):
+            z_copy(q, d).start()
+
+    lead_own.wait()
+    for d in range(1, n_col):
+        lead_copy(d).wait_recv()
+
+    @pl.loop(0, n_row)
+    def _(b):
+        strip_send[b] = lead_recv[pick[GROUPS + b]]
+
+    for e in range(1, n_row):
+        for whole in (False, True):
+            strip_copy(e, whole).start()
+    strip[r] = strip_send[r]
+    corner_strip[r] = strip_send[0]
+    z_start(0)
+    z_start(1)
+    for e in range(1, n_row):
+        for whole in (False, True):
+            kind, peer = int(whole), row_peer(e)
+            remote(
+                strip_send.at[0], corner_strip.at[peer], strip_sent.at[kind, e], strip_got.at[kind, peer], {"row": peer}
+            ).wait_recv()
+            remote(
+                lead_front.at[0], corner_front.at[peer], front_send.at[kind, e], front_got.at[kind, peer], {"row": peer}
+            ).wait_recv()
+
+    @pl.loop(0, NB)
+    def _(j):
+        tile = strip_front[j % 8, j // 8]
+        for child in range(2):
+            part = strip[src_row[child, j], src_tile[child, j]].astype(jnp.float32)
+            tile = tile + jnp.where(valid[child] > 0, part, 0.0)
+        mine[pl.ds(pl.multiple_of(j * T, T), T), :] = tile
+
+    move = remote(
+        mine, moved, move_sem.at[0], move_sem.at[1], {"row": target_row, "col": target_col}
+    )
+    move_own = pltpu.make_async_copy(mine, moved, move_sem.at[2])
+
+    @pl.when(moves)
+    def _():
+        move.start()
+
+    @pl.when(jnp.logical_not(moves))
+    def _():
+        move_own.start()
+
+    @pl.loop(0, CORNER)
+    def _(t):
+        j = lax.rem(c + t, NB)
+        tile = corner_front[j % 8, j // 8]
+        for child in range(2):
+            tile = tile + corner_strip[src_row[child, j], src_tile[child, j]].astype(jnp.float32)
+        corner[c, pl.ds(pl.multiple_of(t * T, T), T), :] = tile
+
+    half_rows = CORNER * T // 2
+    part_rows = half_rows // 2
+    ring, twins = [], []
+
+    def place(part, along, across):
+        return at_col(across, along) if part == 0 else at_col(along, across)
+
+    def piece(block, part, owner):
+        return corner.at[block, pl.ds(pl.multiple_of(owner * half_rows + part * part_rows, part_rows), part_rows)]
+
+    def ring_copy(block, part, target):
+        ref = piece(block, part, core)
+        copy = remote(ref, ref, ring_send.at[len(ring)], ring_got.at[block, part], {"col": target})
+        copy.start()
+        ring.append(copy)
+
+    def ring_wait(block, part):
+        ref = piece(block, part, core)
+        remote(ref, ref, ring_send.at[0], ring_got.at[block, part], {"col": at_col(1, 0)}).wait_recv()
+        copy = remote(ref, ref, twin_send.at[len(twins)], twin_got.at[block, part], {"row": twin})
+        copy.start()
+        twins.append(copy)
+
+    for part in range(2):
+        ring_copy(c, part, place(part, 1, 0))
+        ring_copy(c, part, place(part, -1, 0))
+    for part in range(2):
+        ring_copy(c, part, place(part, 0, 1))
+        ring_copy(c, part, place(part, 0, -1))
+    for part in range(2):
+        block = place(part, -step, 0)
+        ring_wait(block, part)
+        ring_copy(block, part, place(part, step, 0))
+        ring_copy(block, part, place(part, 0, 1))
+        ring_copy(block, part, place(part, 0, -1))
+    for part in range(2):
+        block = place(part, step, 0)
+        ring_wait(block, part)
+        ring_copy(block, part, place(part, 0, 1))
+        ring_copy(block, part, place(part, 0, -1))
+    for part in range(2):
+        block = place(part, 2, 0)
+        ring_wait(block, part)
+        ring_copy(block, part, place(part, 0, 1))
+        ring_copy(block, part, place(part, 0, -1))
+    for along in (0, -step, step, 2):
+        for part in range(2):
+            block = place(part, along, -step)
+            ring_wait(block, part)
+            ring_copy(block, part, place(part, 0, step))
+    for along in range(4):
+        for across in (step, 2):
+            for part in range(2):
+                ring_wait(place(part, along, across), part)
+    z_start(2)
+    z_start(3)
     mat[...] = jnp.zeros_like(mat)
-    for d in range(NB // 2 + 1):
+    mat[:, NB * T : NB * T + T] = mine[...]
+
+    @pl.when(moves)
+    def _():
+        move.wait()
+
+    @pl.when(jnp.logical_not(moves))
+    def _():
+        move_own.wait()
+
+    mat[:, NB * T + T :] = moved[...]
+    for dx in range(4):
+        for dz in range(4):
+            if dx or dz:
+                for part in range(2):
+                    block = at_col(dx, dz)
+                    ref = piece(block, part, 1 - core)
+                    remote(ref, ref, twin_send.at[0], twin_got.at[block, part], {"row": twin}).wait_recv()
+
+    for d in range(NB):
         for i in range(d, NB):
-            tile = lead[i - d, d] if d < 6 else lead[i, 6]
-            mat[(i - d) * T : (i - d + 1) * T, i * T : (i + 1) * T] = tile.T if 0 < d < 6 else tile
-    for d in range(7, NB):
-        for i in range(d, NB):
-            mat[(i - d) * T : (i - d + 1) * T, i * T : (i + 1) * T] = lead[i, NB - d]
-    mat[:, NB * T :] = rhs[...]
+            if d < 6:
+                tile = corner[i - d, d * T : (d + 1) * T, :]
+                tile = tile.T if d else tile
+            else:
+                tile = corner[i, (NB - d) * T : (NB - d + 1) * T, :]
+            mat[(i - d) * T : (i - d + 1) * T, i * T : (i + 1) * T] = tile
     row_id = lax.broadcasted_iota(jnp.int32, (T, T), 0)
     col_id = lax.broadcasted_iota(jnp.int32, (T, T), 1)
     chunks = WIDE // 256
@@ -160,16 +351,34 @@
 
         for q in range(Q):
 
-            @pl.when(k == (q + 1) * (NB // Q) - 1)
+            @pl.when(k == X_START[q])
             def _(q=q):
-                col_own(q).wait()
-                for d in range(1, n_col):
-                    col_copy(q, d).wait_recv()
+                z_own(q).wait()
+                for d in range(1, 4):
+                    z_copy(q, d).wait_recv()
+
+                @pl.loop(0, REST)
+                def _(i):
+                    for kind in range(4):
+                        for d in range(4):
+                            into = x_recv[q] if d == 0 else x_out[q]
+                            into[d, kind, i] = z_recv[q][kind, pair[d, kind], i]
+
+                for d in range(1, 4):
+                    x_copy(q, d).start()
+
+            @pl.when(k == ROW_START[q])
+            def _(q=q):
+                for d in range(1, 4):
+                    x_copy(q, d).wait_recv()
 
                 @pl.loop(0, n_row * 4)
                 def _(i):
+                    line = turn[i]
                     for g in range(GROUPS):
-                        packed[q, i // 4, i % 4, g] = recv[q][pick[g], turn[i]]
+                        rest = x_recv[q][pick[16 + g], pick[24 + g], jnp.minimum(line, REST - 1)]
+                        first = lead_recv[pick[g], jnp.maximum(line - REST, 0), q * PART : (q + 1) * PART]
+                        packed[q, i // 4, i % 4, g] = jnp.where(line < REST, rest, first)
 
                 row_own(q).start()
                 for e in range(1, n_row):
@@ -177,45 +386,78 @@
 
     out[...] = mat[:, NB * T :]
 
+    for d in range(1, n_col):
+        lead_copy(d).wait_send()
+    for e in range(1, n_row):
+        for whole in (False, True):
+            front_copy(e, whole).wait_send()
+            strip_copy(e, whole).wait_send()
+    for copy in ring + twins:
+        copy.wait_send()
     for q in range(Q):
         row_own(q).wait()
-        for d in range(1, n_col):
-            col_copy(q, d).wait_send()
+        for d in range(1, 4):
+            z_copy(q, d).wait_send()
+            x_copy(q, d).wait_send()
         for e in range(1, n_row):
             row_copy(q, e).wait()
 
 
-def exchange_factor(pick, turn, slots, lead, rhs):
+def exchange_factor(tables, lead_slots, slots, lead_front):
     n_row, n_col = lax.axis_size("row"), lax.axis_size("col")
     vmem = pl.BlockSpec(memory_space=pltpu.VMEM)
     smem = pl.BlockSpec(memory_space=pltpu.SMEM)
     hbm = pl.BlockSpec(memory_space=pl.ANY)
     dma = pltpu.SemaphoreType.DMA
+    f32, bf16 = jnp.float32, jnp.bfloat16
     return pl.pallas_call(
         exchange_factor_kernel,
         out_shape=(
-            jax.ShapeDtypeStruct((NB * T, RHS), jnp.float32),
-            jax.ShapeDtypeStruct((Q, n_row, 4, GROUPS, PART, T), jnp.bfloat16),
+            jax.ShapeDtypeStruct((NB * T, RHS), f32),
+            jax.ShapeDtypeStruct((Q, n_row, 4, GROUPS, PART, T), bf16),
         ),
-        in_specs=[smem, smem, hbm, vmem, vmem],
+        in_specs=[smem] * 6 + [hbm, hbm, vmem],
         out_specs=(vmem, hbm),
         scratch_shapes=[
-            pltpu.VMEM((NB * T, WIDE), jnp.float32),
-            pltpu.VMEM((T, 2 * T), jnp.float32),
-            pltpu.VMEM((T, T), jnp.float32),
-            pltpu.VMEM((T, 256), jnp.float32),
-            pltpu.VMEM((Q, n_row, 4, GROUPS, PART, T), jnp.bfloat16),
-            dma((2 * Q,)),
-            dma((Q, n_col)),
-            dma((Q, n_col)),
+            pltpu.VMEM((NB * T, WIDE), f32),
+            pltpu.VMEM((T, 2 * T), f32),
+            pltpu.VMEM((T, T), f32),
+            pltpu.VMEM((T, 256), f32),
+            pltpu.VMEM((Q, n_row, 4, GROUPS, PART, T), bf16),
+            pltpu.VMEM((n_col, LEAD_ROWS, T, T), bf16),
+            pltpu.VMEM((n_row, LEAD_ROWS, T, T), bf16),
+            pltpu.VMEM((n_row, LEAD_ROWS, T, T), bf16),
+            pltpu.VMEM((n_row, LEAD_ROWS, T, T), bf16),
+            pltpu.VMEM((n_row, 2, T, T), f32),
+            pltpu.VMEM((n_row, 2, T, T), f32),
+            pltpu.VMEM((NB * T, T), f32),
+            pltpu.VMEM((NB * T, T), f32),
+            pltpu.VMEM((n_col, CORNER * T, T), f32),
+            dma((1 + 2 * Q,)),
+            dma((n_col,)),
+            dma((n_col,)),
+            dma((2, n_row)),
+            dma((2, n_row)),
+            dma((2, n_row)),
+            dma((2, n_row)),
+            dma((3,)),
+            dma((32,)),
+            dma((n_col, 2)),
+            dma((32,)),
+            dma((n_col, 2)),
+            dma((Q, 4)),
+            dma((Q, 4)),
+            dma((Q, 4)),
+            dma((Q, 4)),
             dma((Q, n_row)),
             dma((Q, n_row)),
         ]
-        + [pltpu.VMEM((n_col, ROWS, PART, T), jnp.bfloat16)] * Q,
+        + [pltpu.VMEM((4, 2, REST, PART, T), bf16)] * Q
+        + [pltpu.VMEM((4, 4, REST, PART, T), bf16)] * (2 * Q),
         compiler_params=pltpu.CompilerParams(
-            vmem_limit_bytes=60 * 1024 * 1024, collective_id=0, has_side_effects=True
+            vmem_limit_bytes=62 * 1024 * 1024, collective_id=0, has_side_effects=True
         ),
-    )(pick, turn, slots, lead, rhs)
+    )(*tables, lead_slots, slots, lead_front)
 
 
 def update_kernel(
@@ -453,10 +695,6 @@
     )(fill, row_pick, col_pick, left, right, got, front)
 
 
-def gather_tiles(tiles, *index):
-    return tiles.at[index].get(mode="promise_in_bounds")
-
-
 def local(front, children, child_maps, fill):
     n_row = lax.axis_size("row")
     n_col = lax.axis_size("col")
@@ -485,51 +723,49 @@
     fill_local = lax.dynamic_index_in_dim(fill_rows, c, 2, keepdims=False).astype(jnp.float32)
     base = own[:2] * fill_local[:2, None, :, None]
 
-    lead_rows = lax.dynamic_slice_in_dim(tiles, per * first[h], per, axis=1)
-    send_group = by_shift[h][(wanted - c) % n_col]
-    lead_got = lax.all_to_all(lead_rows[send_group], "col", 0, 0, tiled=True)
-    parts = tiles.reshape(groups, child_rows, Q, PART, T).transpose(2, 0, 1, 3, 4)
-    slots = parts[:, by_shift[h]]
-
-    own_blocks = by_block[h]
-    source = (c - shifts[h][own_blocks]) % n_col
-    lead_blocks = jnp.where(has_block[h][:, None, None, None], lead_got[source], 0)
-    strip = lax.all_to_all(lead_blocks, "row", 0, 0, tiled=True).reshape(n_row, per, T, T)
+    lead_tiles = lax.dynamic_slice_in_dim(tiles, per * first[h], per, axis=1)
+    lead_slots = lead_tiles[by_shift[h]]
     lead_front = base.transpose(2, 0, 1, 3)
-    strip_front = lax.all_to_all(lead_front, "row", 0, 0, tiled=True)
-    lead_gather = lax.all_gather(lead_blocks[0], "row", axis=0)
-    front_gather = lax.all_gather(lead_front[0], "row", axis=0)
-
-    def lead_column(parts, fronts):
-        total = fronts.transpose(1, 0, 2, 3).reshape(n_col, T, T)
-        for child in range(2):
-            places = (wanted - shifts[child, first[child]]) % n_col
-            total += parts[child * half + places % half, places // half].astype(jnp.float32)
-        return total
-
-    mine = lead_column(strip, strip_front)[:NB].reshape(NB * T, T)
-    corner = lead_column(lead_gather, front_gather)[:NB]
-    corner = corner[(c + jnp.arange(NB // 2 + 1)) % NB]
-    lead = lax.all_gather(corner, "col", axis=0)
-    pairs = [(i * n_col + j, (j % n_row) * n_col + 2 * i + j // n_row) for i in range(n_row) for j in range(n_col)]
-    moved = lax.ppermute(mine, ("row", "col"), pairs)
+
     ranks = jnp.sum(
         (shifts[:, None, :] % half == shifts[:, :, None] % half)
         & (jnp.arange(groups)[None, None, :] < jnp.arange(groups)[None, :, None]),
         axis=2,
     )
+    my_shifts, my_ranks = shifts[h], ranks[h]
+    kinds = my_shifts % 4
+    chosen = (kinds[None, None, :] == jnp.arange(4)[:, None, None]) & (
+        my_ranks[None, None, :] == jnp.arange(2)[None, :, None]
+    )
+    by_kind = jnp.argmax(chosen, axis=2)
+    lines = (per * (first[h] + 1) + jnp.arange(REST)) % child_rows
+    slots = tiles[by_kind[:, :, None], lines[None, None, :]]
+    slots = slots.reshape(4, 2, REST, Q, PART, T).transpose(3, 0, 1, 2, 4, 5)
+    x, z = c // 4, c % 4
+    hops = (my_shifts // 4 + (z < kinds)) % 4
+    pair = jnp.sum(
+        jnp.where(
+            (hops[None, None, :] == jnp.arange(4)[:, None, None])
+            & (kinds[None, None, :] == jnp.arange(4)[None, :, None]),
+            my_ranks[None, None, :],
+            0,
+        ),
+        axis=2,
+    )
+    pad = jnp.zeros((2,), jnp.int32)
+    pick = jnp.concatenate(
+        [my_shifts, my_shifts[by_block[h]], pad, hops, pad, kinds]
+    ).astype(jnp.int32)
+    places = (wanted[None, :NB] - jnp.take_along_axis(shifts, first[:, None], axis=1)) % n_col
+    src_row = half * jnp.arange(2)[:, None] + places % half
     rows = (r + jnp.arange(n_row)) % n_row
-    lanes = (lane + shifts[h][None, :]) % half == (rows % half)[:, None]
-    choice = jnp.argmax(lanes[:, None, :] & (ranks[h][None, None, :] == jnp.arange(2)[None, :, None]), axis=2)
-    turn = (rows[:, None, None] + n_row * jnp.arange(2)[None, None, :] - lane - shifts[h][choice][:, :, None]) % n_col
+    lanes = (lane + my_shifts[None, :]) % half == (rows % half)[:, None]
+    choice = jnp.argmax(lanes[:, None, :] & (my_ranks[None, None, :] == jnp.arange(2)[None, :, None]), axis=2)
+    turn = (rows[:, None, None] + n_row * jnp.arange(2)[None, None, :] - lane - my_shifts[choice][:, :, None]) % n_col
     turn = (per * choice[:, :, None] + turn // half).reshape(4 * n_row)
-    solved, got = exchange_factor(
-        shifts[h].astype(jnp.int32),
-        turn.astype(jnp.int32),
-        slots,
-        lead,
-        jnp.concatenate([mine, moved], axis=1),
-    )
+    turn = (turn - per * (first[h] + 1)) % child_rows
+    tables = [pick, turn, pair, src_row, places // half, has_block[:, r]]
+    solved, got = exchange_factor([t.astype(jnp.int32) for t in tables], lead_slots, slots, lead_front)
 
     exponent = jnp.floor(jnp.log2(jnp.maximum(jnp.max(jnp.abs(solved), axis=0), 1e-30))) + 1.0
     coded = jnp.clip(jnp.round(solved * jnp.exp2(15.0 - exponent)), -32767.0, 32767.0).astype(jnp.int16)

time: 537 us -> 455 us (0.85)
  waiting for transfers between devices: 110 us -> 0 us
  Pallas kernels: 311 us -> 391 us
  between operations: 19 us -> 1.54 us
  local copies, waits for them, and re-layouts: 62.9 us -> 46.7 us
  starting transfers between devices: 16.1 us -> 0 us
    pallas_call x1, Pallas kernels: 215 us -> 303 us  [exchange_factor(): pl.pallas_call(exchange_factor_kernel, out_shape=(jax.ShapeDtypeStruct((N...]
    all_to_all x3 -> x0, waiting for transfers between devices: 55.9 us -> none  [the longest x1 29.6 us: local(): lead_got = lax.all_to_all(lead_rows[send_group], 'col', 0, 0, tiled=True)]
    all_gather x3 -> x0, waiting for transfers between devices: 54.2 us -> none  [the longest x1 21.2 us: local(): front_gather = lax.all_gather(lead_front[0], 'row', axis=0)]
    all_to_all x3 -> x0, starting transfers between devices: 15.1 us -> none  [the longest x1 7.96 us: local(): lead_got = lax.all_to_all(lead_rows[send_group], 'col', 0, 0, tiled=True)]
    gather x13 -> x8, local copies, waits for them, and re-layouts: 33.2 us -> 19 us  [the longest x1 14.6 us: local(): slots = tiles[by_kind[:, :, None], lines[None, None, :]]]
    pallas_call x1, Pallas kernels: 95.5 us -> 87.5 us  [update(): pl.pallas_call(update_kernel, out_shape=jax.ShapeDtypeStruct(front.shape,...]
  transfers between devices with their start and end apart: 7 -> 0, of which waited for: 6 -> 0; matrix products, arithmetic and copies ran while one was open for 10% -> 0% of each run, Pallas kernels for 0% -> 0%
where the time goes in v3:
time: 455 us; the launch traced here: 450 us
  Pallas kernels  391 us (86%)
  local copies, waits for them, and re-layouts  46.7 us (10%)
  other arithmetic  11.2 us (2%)
    pallas_call x1, Pallas kernels, exchange_factor(): pl.pallas_call(exchange_factor_kernel, out_shape=(jax.ShapeDtypeStruct((N...  303 us
    pallas_call x1, Pallas kernels, update(): pl.pallas_call(update_kernel, out_shape=jax.ShapeDtypeStruct(front.shape,...  87.5 us
    gather x1, local copies, waits for them, and re-layouts, local(): slots = tiles[by_kind[:, :, None], lines[None, None, :]]  14.6 us

profile of v3, /device:TPU:0, one launch (start us, length us, event | category | flops | bytes accessed | tf_op | source)
XLA Modules:
  0.0 450.1 jit_solution(5849076220769307279)
XLA Ops:
  0.0 0.8 slice.57
  1.0 0.1 fusion.38
  1.1 0.1 copy.36
  1.2 0.5 iota_reduce_fusion
  1.8 0.1 fusion.35
  1.9 0.1 copy.41
  2.0 0.7 fusion.6
  2.8 0.6 gather_fusion.12
  3.4 0.1 copy.42
  3.5 0.1 fusion.10
  3.6 0.7 and_select_fusion.1
  4.3 0.5 pad_add_fusion.2.col_pick
  4.8 0.5 fusion.42
  6.8 0.1 copy.43
  6.9 0.6 compare_reduce_fusion
  7.5 0.7 gather_fusion.7
  8.1 0.7 gather_fusion.6
  8.8 0.7 gather_fusion.2
  9.5 0.7 gather_fusion
  10.2 0.7 gather_fusion.3
  10.9 0.7 gather_fusion.1
  11.6 0.6 gather_fusion.8
  12.2 0.6 concatenate.16.pick
  12.9 0.1 copy.37
  12.9 0.2 fusion.2
  13.2 0.2 dynamic-slice_reduce_fusion
  13.4 0.7 gather_fusion.4
  14.1 0.7 gather_fusion.5
  14.8 0.7 select_reduce_fusion.pair
  15.5 0.1 copy.38
  15.6 0.6 and_reduce_fusion
  16.2 0.6 iota_reduce_fusion.1
  16.8 0.1 copy.44
  16.9 0.6 stack.2.row_pick
  17.6 0.1 reshape.896
  17.7 0.1 copy.40
  17.8 0.1 reshape.882
  17.9 0.7 gather_fusion.9
  18.5 0.1 reshape.881
  18.6 0.1 broadcast_subtract_fusion
  18.7 0.1 sub.159
  18.8 0.1 copy.39
  18.9 0.1 add.486
  19.0 0.1 add.487
  19.1 0.6 and_select_fusion.5.turn
  19.7 0.2 reshape.800
  19.9 0.1 constant_dynamic-slice_fusion.5
  20.0 0.2 copy.50
  20.1 0.7 convert_element_type.59.fill
  20.8 0.1 copy.47
  20.9 1.2 dynamic-slice_bitcast_fusion
  22.1 1.3 slice.68
  23.4 1.2 fusion.1.lead_front
  24.6 2.2 gather_fusion.10
  26.8 14.6 %gather_fusion.11 = bf16[160,128,128]{2,1,0:T(8,128)(2,1)} fusion(bf16[6,24,128,128]{3,2,0,1:T(8,128)(2,1)} %bitcast.102, s32[160]{0:T(256)S(1)} %reshape.896), kind=kCustom, calls=%fused_computation.11 | custom fusion | bytes 10487040 | tf_op jit(solution)/shard_map/gather | solution.py:742
  41.4 6.4 %copy.58 = bf16[4,2,20,4,32,128]{5,4,2,1,0,3:T(8,128)(2,1)} copy(bf16[4,2,20,4,32,128]{5,4,3,2,1,0:T(8,128)(2,1)} %bitcast.100) | data formatting | bytes 10485760 | tf_op jit(solution)/shard_map/reshape | solution.py:743
  47.8 303.2 %shard_map.46 = (f32[1536,256]{1,0:T(8,128)}, bf16[4,8,4,6,32,128]{5,4,3,2,1,0:T(8,128)(2,1)}) custom-call(s32[30]{0:T(128)} %concatenate.16.pick, s32[32]{0:T(128)} %and_select_fusion.5.turn, s32[4,4]{1,0:T(4,128)} %select_reduce_fusion.pair, s32[2,12]{1,0:T(2,128)} %get-tuple-element.30.src_row, s32[2,12]{1,0:T(2,128)} %get-tuple-element.29.src_tile, ...), custom_call_target="tpu_custom_call" | custom-call | tf_op jit(solution)/shard_map/pallas_call | solution.py:413
  351.0 1.6 abs_reduce_fusion
  352.6 0.2 copy-done
  352.9 0.2 clamp_convert_fusion
  353.2 0.8 pad_add_fusion.1.right
  354.0 1.1 copy.48.left
  355.1 87.5 %shard_map.47 = f32[16384,128]{1,0:T(8,128)} custom-call(f32[128]{0:T(128)} %convert_element_type.59.fill, s32[6,16]{1,0:T(8,128)} %stack.2.row_pick, s32[4,8]{1,0:T(4,128)} %pad_add_fusion.2.col_pick, s16[128,1664]{1,0:T(8,128)(2,1)} %copy.48.left, s16[1552,128]{1,0:T(8,128)(2,1)} %pad_add_fusion.1.right, ...), custom_call_target="tpu_custom_call" | custom-call | tf_op jit(solution)/shard_map/pallas_call | solution.py:674
  442.5 7.6 %copy.60 = f32[1,16,128,1,8,128]{5,4,3,2,1,0:T(8,128)} copy(f32[1,16,128,1,8,128]{5,4,3,2,1,0:T(8,128)} %bitcast.98) | data formatting | bytes 16777216
  (47 shorter events, 0.6 us)
Async XLA Ops:
  17.9 1.8 copy-start.1
  351.0 1.9 copy-start

commit v4 on v3

--- a/solution.py
+++ b/solution.py
@@ -72,13 +72,13 @@
 
 
 def exchange_factor_kernel(
-    pick, turn, pair, src_row, src_tile, valid, lead_slots, slots, lead_front, out, got,
-    mat, work, winv, acc, packed, lead_recv, strip_send, strip, corner_strip, strip_front, corner_front,
+    pick, turn, pair, src_row, src_tile, valid, by_shift, by_kind, first, tiles, lead_front, out, got,
+    mat, work, winv, acc, packed, lead_slots, z_out, lead_recv, strip, corner_strip, strip_front, corner_front,
     mine, moved, corner, own_sem, lead_send, lead_got, front_send, front_got, strip_sent, strip_got,
-    move_sem, ring_send, ring_got, twin_send, twin_got, z_send, z_got, x_send, x_got, row_send, row_got, *buffers,
+    move_send, move_got, ring_send, ring_got, twin_send, twin_got, z_send, z_got, x_send, x_got, row_send, row_got, *buffers,
 ):
     n_row, n_col = lax.axis_size("row"), lax.axis_size("col")
-    z_recv, x_out, x_recv = buffers[:Q], buffers[Q : 2 * Q], buffers[2 * Q :]
+    z_recv, x_recv, x_out = buffers[:Q], buffers[Q : 2 * Q], buffers[2 * Q :]
     r, c = lax.axis_index("row"), lax.axis_index("col")
     x, z = c // 4, c % 4
     core = r % 2
@@ -131,68 +131,78 @@
     def strip_copy(e, whole):
         if whole:
             return remote(
-                strip_send.at[0], corner_strip.at[r], strip_sent.at[1, e], strip_got.at[1, r], {"row": row_peer(e)}
+                lead_slots.at[0], corner_strip.at[r], strip_sent.at[1, e], strip_got.at[1, r], {"row": row_peer(e)}
             )
         return remote(
-            strip_send.at[row_peer(e)], strip.at[r], strip_sent.at[0, e], strip_got.at[0, r], {"row": row_peer(e)}
-        )
-
-    lead_own = pltpu.make_async_copy(lead_slots.at[0], lead_recv.at[0], own_sem.at[0])
-    lead_own.start()
-    for d in range(1, n_col):
-        lead_copy(d).start()
+            lead_slots.at[row_peer(e)], strip.at[r], strip_sent.at[0, e], strip_got.at[0, r], {"row": row_peer(e)}
+        )
+
     for e in range(1, n_row):
         for whole in (False, True):
             front_copy(e, whole).start()
+
+    @pl.loop(0, n_col)
+    def _(d):
+        for i in range(LEAD_ROWS):
+            lead_slots[d, i] = tiles[LEAD_ROWS * first[0] + i, by_shift[d]]
+
+    for d in range(1, n_col):
+        lead_copy(d).start()
+    lead_recv[0] = lead_slots[0]
     strip_front[r] = lead_front[r]
     corner_front[r] = lead_front[0]
 
     def z_copy(q, d):
         return remote(
-            slots.at[q, d], z_recv[q].at[d], z_send.at[q, d], z_got.at[q, d], {"col": at_col(0, d)}
-        )
-
-    def z_own(q):
-        return pltpu.make_async_copy(slots.at[q, 0], z_recv[q].at[0], own_sem.at[1 + q])
+            z_out.at[q, d - 1], z_recv[q].at[d], z_send.at[q, d], z_got.at[q, d], {"col": at_col(0, d)}
+        )
 
     def x_copy(q, d):
         return remote(
-            x_out[q].at[d], x_recv[q].at[d], x_send.at[q, d], x_got.at[q, d], {"col": at_col(d, 0)}
+            x_out[q % 2].at[d - 1], x_recv[q].at[d], x_send.at[q, d], x_got.at[q, d], {"col": at_col(d, 0)}
         )
 
     def row_copy(q, e):
         return remote(
-            packed.at[q, e], got.at[q, e], row_send.at[q, e], row_got.at[q, e], {"row": row_peer(e)}
+            packed.at[e], got.at[q, e], row_send.at[q, e], row_got.at[q, e], {"row": row_peer(e)}
         )
 
     def row_own(q):
-        return pltpu.make_async_copy(packed.at[q, 0], got.at[q, 0], own_sem.at[1 + Q + q])
+        return pltpu.make_async_copy(packed.at[0], got.at[q, 0], own_sem.at[q])
 
     def z_start(q):
-        z_own(q).start()
         for d in range(1, 4):
             z_copy(q, d).start()
 
-    lead_own.wait()
+    @pl.loop(0, REST)
+    def _(i):
+        line = lax.rem(LEAD_ROWS * (first[0] + 1) + i, LEAD_ROWS + REST)
+        for a in range(2):
+            for q in range(Q):
+                part = slice(q * PART, (q + 1) * PART)
+                z_recv[q][0, a, i] = tiles[line, by_kind[0, a], part]
+                for d in range(1, 4):
+                    z_out[q, d - 1, a, i] = tiles[line, by_kind[d, a], part]
+
     for d in range(1, n_col):
-        lead_copy(d).wait_recv()
+        lead_copy(d).wait()
 
     @pl.loop(0, n_row)
     def _(b):
-        strip_send[b] = lead_recv[pick[GROUPS + b]]
+        lead_slots[b] = lead_recv[pick[GROUPS + b]]
 
     for e in range(1, n_row):
         for whole in (False, True):
             strip_copy(e, whole).start()
-    strip[r] = strip_send[r]
-    corner_strip[r] = strip_send[0]
+    strip[r] = lead_slots[r]
+    corner_strip[r] = lead_slots[0]
     z_start(0)
     z_start(1)
     for e in range(1, n_row):
         for whole in (False, True):
             kind, peer = int(whole), row_peer(e)
             remote(
-                strip_send.at[0], corner_strip.at[peer], strip_sent.at[kind, e], strip_got.at[kind, peer], {"row": peer}
+                lead_slots.at[0], corner_strip.at[peer], strip_sent.at[kind, e], strip_got.at[kind, peer], {"row": peer}
             ).wait_recv()
             remote(
                 lead_front.at[0], corner_front.at[peer], front_send.at[kind, e], front_got.at[kind, peer], {"row": peer}
@@ -206,18 +216,11 @@
             tile = tile + jnp.where(valid[child] > 0, part, 0.0)
         mine[pl.ds(pl.multiple_of(j * T, T), T), :] = tile
 
-    move = remote(
-        mine, moved, move_sem.at[0], move_sem.at[1], {"row": target_row, "col": target_col}
-    )
-    move_own = pltpu.make_async_copy(mine, moved, move_sem.at[2])
-
-    @pl.when(moves)
-    def _():
-        move.start()
-
-    @pl.when(jnp.logical_not(moves))
-    def _():
-        move_own.start()
+    def move(k):
+        rows = pl.ds(pl.multiple_of(k * T, T), T)
+        return remote(
+            mine.at[rows], moved.at[rows], move_send.at[k], move_got.at[k], {"row": target_row, "col": target_col}
+        )
 
     @pl.loop(0, CORNER)
     def _(t):
@@ -281,20 +284,21 @@
         for across in (step, 2):
             for part in range(2):
                 ring_wait(place(part, along, across), part)
+    @pl.when(moves)
+    def _():
+        @pl.loop(0, NB)
+        def _(k):
+            move(k).start()
+
     z_start(2)
     z_start(3)
     mat[...] = jnp.zeros_like(mat)
     mat[:, NB * T : NB * T + T] = mine[...]
 
-    @pl.when(moves)
-    def _():
-        move.wait()
-
     @pl.when(jnp.logical_not(moves))
     def _():
-        move_own.wait()
-
-    mat[:, NB * T + T :] = moved[...]
+        mat[:, NB * T + T :] = mine[...]
+
     for dx in range(4):
         for dz in range(4):
             if dx or dz:
@@ -320,6 +324,11 @@
         k0 = pl.multiple_of(k * T, T)
         kk = pl.ds(k0, T)
 
+        @pl.when(moves)
+        def _():
+            move(k).wait_recv()
+            mat[kk, NB * T + T :] = moved[kk, :]
+
         @pl.loop(k // 2, chunks)
         def _(n):
             nn = pl.ds(pl.multiple_of(n * 256, 256), 256)
@@ -353,16 +362,20 @@
 
             @pl.when(k == X_START[q])
             def _(q=q):
-                z_own(q).wait()
                 for d in range(1, 4):
                     z_copy(q, d).wait_recv()
+                    if q >= 2:
+                        x_copy(q - 2, d).wait_send()
 
                 @pl.loop(0, REST)
                 def _(i):
                     for kind in range(4):
                         for d in range(4):
-                            into = x_recv[q] if d == 0 else x_out[q]
-                            into[d, kind, i] = z_recv[q][kind, pair[d, kind], i]
+                            tile = z_recv[q][kind, pair[d, kind], i]
+                            if d == 0:
+                                x_recv[q][d, kind, i] = tile
+                            else:
+                                x_out[q % 2][d - 1, kind, i] = tile
 
                 for d in range(1, 4):
                     x_copy(q, d).start()
@@ -371,6 +384,10 @@
             def _(q=q):
                 for d in range(1, 4):
                     x_copy(q, d).wait_recv()
+                if q >= 1:
+                    row_own(q - 1).wait()
+                    for e in range(1, n_row):
+                        row_copy(q - 1, e).wait_send()
 
                 @pl.loop(0, n_row * 4)
                 def _(i):
@@ -378,7 +395,7 @@
                     for g in range(GROUPS):
                         rest = x_recv[q][pick[16 + g], pick[24 + g], jnp.minimum(line, REST - 1)]
                         first = lead_recv[pick[g], jnp.maximum(line - REST, 0), q * PART : (q + 1) * PART]
-                        packed[q, i // 4, i % 4, g] = jnp.where(line < REST, rest, first)
+                        packed[i // 4, i % 4, g] = jnp.where(line < REST, rest, first)
 
                 row_own(q).start()
                 for e in range(1, n_row):
@@ -386,8 +403,6 @@
 
     out[...] = mat[:, NB * T :]
 
-    for d in range(1, n_col):
-        lead_copy(d).wait_send()
     for e in range(1, n_row):
         for whole in (False, True):
             front_copy(e, whole).wait_send()
@@ -395,15 +410,26 @@
     for copy in ring + twins:
         copy.wait_send()
     for q in range(Q):
-        row_own(q).wait()
         for d in range(1, 4):
             z_copy(q, d).wait_send()
-            x_copy(q, d).wait_send()
+        if q >= 2:
+            for d in range(1, 4):
+                x_copy(q, d).wait_send()
+        if q == Q - 1:
+            row_own(q).wait()
+            for e in range(1, n_row):
+                row_copy(q, e).wait_send()
         for e in range(1, n_row):
-            row_copy(q, e).wait()
-
-
-def exchange_factor(tables, lead_slots, slots, lead_front):
+            row_copy(q, e).wait_recv()
+
+    @pl.when(moves)
+    def _():
+        @pl.loop(0, NB)
+        def _(k):
+            move(k).wait_send()
+
+
+def exchange_factor(tables, tiles, lead_front):
     n_row, n_col = lax.axis_size("row"), lax.axis_size("col")
     vmem = pl.BlockSpec(memory_space=pltpu.VMEM)
     smem = pl.BlockSpec(memory_space=pltpu.SMEM)
@@ -416,16 +442,17 @@
             jax.ShapeDtypeStruct((NB * T, RHS), f32),
             jax.ShapeDtypeStruct((Q, n_row, 4, GROUPS, PART, T), bf16),
         ),
-        in_specs=[smem] * 6 + [hbm, hbm, vmem],
+        in_specs=[smem] * 9 + [vmem, vmem],
         out_specs=(vmem, hbm),
         scratch_shapes=[
             pltpu.VMEM((NB * T, WIDE), f32),
             pltpu.VMEM((T, 2 * T), f32),
             pltpu.VMEM((T, T), f32),
             pltpu.VMEM((T, 256), f32),
-            pltpu.VMEM((Q, n_row, 4, GROUPS, PART, T), bf16),
+            pltpu.VMEM((n_row, 4, GROUPS, PART, T), bf16),
             pltpu.VMEM((n_col, LEAD_ROWS, T, T), bf16),
-            pltpu.VMEM((n_row, LEAD_ROWS, T, T), bf16),
+            pltpu.VMEM((Q, 3, 2, REST, PART, T), bf16),
+            pltpu.VMEM((n_col, LEAD_ROWS, T, T), bf16),
             pltpu.VMEM((n_row, LEAD_ROWS, T, T), bf16),
             pltpu.VMEM((n_row, LEAD_ROWS, T, T), bf16),
             pltpu.VMEM((n_row, 2, T, T), f32),
@@ -433,14 +460,15 @@
             pltpu.VMEM((NB * T, T), f32),
             pltpu.VMEM((NB * T, T), f32),
             pltpu.VMEM((n_col, CORNER * T, T), f32),
-            dma((1 + 2 * Q,)),
+            dma((Q,)),
             dma((n_col,)),
             dma((n_col,)),
             dma((2, n_row)),
             dma((2, n_row)),
             dma((2, n_row)),
             dma((2, n_row)),
-            dma((3,)),
+            dma((NB,)),
+            dma((NB,)),
             dma((32,)),
             dma((n_col, 2)),
             dma((32,)),
@@ -453,11 +481,12 @@
             dma((Q, n_row)),
         ]
         + [pltpu.VMEM((4, 2, REST, PART, T), bf16)] * Q
-        + [pltpu.VMEM((4, 4, REST, PART, T), bf16)] * (2 * Q),
+        + [pltpu.VMEM((4, 4, REST, PART, T), bf16)] * Q
+        + [pltpu.VMEM((3, 4, REST, PART, T), bf16)] * 2,
         compiler_params=pltpu.CompilerParams(
             vmem_limit_bytes=62 * 1024 * 1024, collective_id=0, has_side_effects=True
         ),
-    )(*tables, lead_slots, slots, lead_front)
+    )(*tables, tiles, lead_front)
 
 
 def update_kernel(
@@ -579,30 +608,16 @@
         wait_left(block, part)
         send_left(block, part, place(part, 0, 1))
         send_left(block, part, place(part, 0, -1))
-    for along in (0, -step, step):
-        for part in range(2):
-            block = place(part, along, -step)
-            wait_left(block, part)
-            send_left(block, part, place(part, 0, step))
     wait_right(at_row(2, False))
     send_right(at_row(2, False), at_row(0, True))
-    assemble(8, 12)
-    for part in range(2):
-        block = place(part, 2, -step)
-        wait_left(block, part)
-        send_left(block, part, place(part, 0, step))
-    assemble(12, 16)
+    assemble(8, 16)
     for dy in range(4):
         wait_right(at_row(dy, True))
-    for along in range(4):
-        for across in (step, 2):
-            for part in range(2):
-                wait_left(place(part, along, across), part)
 
     def split(coded, scale):
         value = coded.astype(jnp.int32).astype(jnp.float32) * scale
         high = value.astype(jnp.bfloat16)
-        return value, high, (value - high.astype(jnp.float32)).astype(jnp.bfloat16)
+        return high, (value - high.astype(jnp.float32)).astype(jnp.bfloat16)
 
     @pl.loop(0, 8)
     def _(j):
@@ -612,29 +627,19 @@
         @pl.loop(0, NB)
         def _(k):
             rows = pl.ds(pl.multiple_of(k * T, T), T)
-            _, high, low = split(rbuf[j, rows, :], scale)
-            rhi[j // 2, rows, lanes] = high
-            rlo[j // 2, rows, lanes] = low
-
-    row_id = lax.broadcasted_iota(jnp.int32, (T, T), 0)
-    col_id = lax.broadcasted_iota(jnp.int32, (T, T), 1)
-    in_panel = c < NB
-    panel_lanes = pl.ds(pl.multiple_of(jnp.minimum(c, NB - 1) * T, T), T)
-
-    @pl.loop(0, 4)
-    def _(s):
-        @pl.loop(0, 4)
-        def _(m):
-            li = s * 4 + m
-            rows = pl.ds(pl.multiple_of(m * T, T), T)
-            scale = jnp.exp2(lbuf[li, :, CODED:LEFT].astype(jnp.int32).astype(jnp.float32) - 15.0)
+            rhi[j // 2, rows, lanes], rlo[j // 2, rows, lanes] = split(rbuf[j, rows, :], scale)
+
+    def subtract(pieces):
+        for m, (li, part) in enumerate(pieces):
+            source = pl.ds(part * 64, 64)
+            scale = jnp.exp2(lbuf[li, source, CODED:LEFT].astype(jnp.int32).astype(jnp.float32) - 15.0)
 
             @pl.loop(0, NB)
-            def _(k):
+            def _(k, m=m, li=li, source=source, scale=scale):
                 lanes = pl.ds(pl.multiple_of(k * T, T), T)
-                _, high, low = split(lbuf[li, :, lanes], scale)
-                lhi[rows, lanes] = high
-                llo[rows, lanes] = low
+                high, low = split(lbuf[li, source, lanes], scale)
+                lhi[m * 64 : (m + 1) * 64, lanes] = high
+                llo[m * 64 : (m + 1) * 64, lanes] = low
 
         @pl.loop(0, 4)
         def _(n):
@@ -642,18 +647,32 @@
             total += jnp.dot(llo[...], rhi[n], preferred_element_type=jnp.float32)
             total += jnp.dot(lhi[...], rhi[n], preferred_element_type=jnp.float32)
             acc[...] = total
-
-            @pl.loop(0, 8)
-            def _(i):
-                m, j = i // 2, i % 2
-                li, lj = s * 4 + m, n * 2 + j
-                row_tile, col_tile = r + 8 * li, c + 16 * lj
-                where = pl.ds(li * T * 8 + lj, T, stride=8)
-                change = acc[pl.ds(pl.multiple_of(m * T, T), T), pl.ds(pl.multiple_of(j * T, T), T)]
-                cleared = (row_tile < NB) & (col_tile >= NB)
-                out[where, :] = jnp.where(cleared, 0.0, out[where, :] - change)
-
-    @pl.when(in_panel)
+            for m, (li, part) in enumerate(pieces):
+                for j in range(2):
+                    lj = n * 2 + j
+                    where = pl.ds((li * T + part * 64) * 8 + lj, 64, stride=8)
+                    change = acc[m * 64 : (m + 1) * 64, j * T : (j + 1) * T]
+                    cleared = (r + 8 * li < NB) & (c + 16 * lj >= NB)
+                    out[where, :] = jnp.where(cleared, 0.0, out[where, :] - change)
+
+    def arrived(across):
+        return [(place(part, along, across), part) for part in range(2) for along in (0, -step, step, 2)]
+
+    subtract(arrived(0))
+    for block, part in arrived(-step):
+        wait_left(block, part)
+        send_left(block, part, place(part, 0, step))
+    subtract(arrived(-step))
+    for across in (step, 2):
+        for block, part in arrived(across):
+            wait_left(block, part)
+        subtract(arrived(across))
+
+    row_id = lax.broadcasted_iota(jnp.int32, (T, T), 0)
+    col_id = lax.broadcasted_iota(jnp.int32, (T, T), 1)
+    panel_lanes = pl.ds(pl.multiple_of(jnp.minimum(c, NB - 1) * T, T), T)
+
+    @pl.when(c < NB)
     def _():
         @pl.loop(0, 16)
         def _(li):
@@ -703,8 +722,8 @@
     c = lax.axis_index("col")
     h = r // half
     lane = r % half
-    tiles = children[0, :, :, 0].transpose(2, 0, 1, 3)
-    groups, child_rows = tiles.shape[:2]
+    tiles = children[0, :, :, 0].transpose(0, 2, 1, 3)
+    child_rows, groups = tiles.shape[:2]
     own = front[0, :, :, 0]
     parent_rows, _, parent_cols, _ = own.shape
     per = n_col // half
@@ -723,8 +742,6 @@
     fill_local = lax.dynamic_index_in_dim(fill_rows, c, 2, keepdims=False).astype(jnp.float32)
     base = own[:2] * fill_local[:2, None, :, None]
 
-    lead_tiles = lax.dynamic_slice_in_dim(tiles, per * first[h], per, axis=1)
-    lead_slots = lead_tiles[by_shift[h]]
     lead_front = base.transpose(2, 0, 1, 3)
 
     ranks = jnp.sum(
@@ -738,9 +755,6 @@
         my_ranks[None, None, :] == jnp.arange(2)[None, :, None]
     )
     by_kind = jnp.argmax(chosen, axis=2)
-    lines = (per * (first[h] + 1) + jnp.arange(REST)) % child_rows
-    slots = tiles[by_kind[:, :, None], lines[None, None, :]]
-    slots = slots.reshape(4, 2, REST, Q, PART, T).transpose(3, 0, 1, 2, 4, 5)
     x, z = c // 4, c % 4
     hops = (my_shifts // 4 + (z < kinds)) % 4
     pair = jnp.sum(
@@ -764,8 +778,8 @@
     turn = (rows[:, None, None] + n_row * jnp.arange(2)[None, None, :] - lane - my_shifts[choice][:, :, None]) % n_col
     turn = (per * choice[:, :, None] + turn // half).reshape(4 * n_row)
     turn = (turn - per * (first[h] + 1)) % child_rows
-    tables = [pick, turn, pair, src_row, places // half, has_block[:, r]]
-    solved, got = exchange_factor([t.astype(jnp.int32) for t in tables], lead_slots, slots, lead_front)
+    tables = [pick, turn, pair, src_row, places // half, has_block[:, r], by_shift[h], by_kind, first[h][None]]
+    solved, got = exchange_factor([t.astype(jnp.int32) for t in tables], tiles, lead_front)
 
     exponent = jnp.floor(jnp.log2(jnp.maximum(jnp.max(jnp.abs(solved), axis=0), 1e-30))) + 1.0
     coded = jnp.clip(jnp.round(solved * jnp.exp2(15.0 - exponent)), -32767.0, 32767.0).astype(jnp.int16)

time: 455 us -> 405 us (0.89)
  Pallas kernels: 391 us -> 367 us
  local copies, waits for them, and re-layouts: 46.7 us -> 23.4 us
    pallas_call x1, Pallas kernels: 303 us -> 280 us  [exchange_factor(): pl.pallas_call(exchange_factor_kernel, out_shape=(jax.ShapeDtypeStruct((N...]
    gather x2 -> x0, local copies, waits for them, and re-layouts: 16.8 us -> none  [the longest x1 14.6 us: local(): slots = tiles[by_kind[:, :, None], lines[None, None, :]]]
    reshape x1 -> x0, local copies, waits for them, and re-layouts: 6.38 us -> none  [local(): slots = slots.reshape(4, 2, REST, Q, PART, T).transpose(3, 0, 1, 2, 4, 5)]
where the time goes in v4:
time: 405 us; the launch traced here: 403 us
  Pallas kernels  367 us (91%)
  local copies, waits for them, and re-layouts  23.4 us (6%)
  other arithmetic  11.2 us (3%)
    pallas_call x1, Pallas kernels, exchange_factor(): pl.pallas_call(exchange_factor_kernel, out_shape=(jax.ShapeDtypeStruct((N...  280 us
    pallas_call x1, Pallas kernels, update(): pl.pallas_call(update_kernel, out_shape=jax.ShapeDtypeStruct(front.shape,...  87.5 us

profile of v4, /device:TPU:0, one launch (start us, length us, event | category | flops | bytes accessed | tf_op | source)
XLA Modules:
  0.0 403.0 jit_solution(545067007013904899)
XLA Ops:
  0.0 0.8 slice.57
  0.9 0.1 broadcast_compare_fusion
  1.0 0.1 fusion.32
  1.1 0.1 copy.34
  1.2 0.5 iota_reduce_fusion
  1.8 0.1 fusion.29
  1.9 0.1 copy.39
  2.0 0.8 fusion.5
  2.8 0.6 gather_fusion.10
  3.4 0.1 copy.40
  3.5 0.1 fusion.7
  3.7 0.7 and_select_fusion
  4.4 0.5 pad_add_fusion.2.col_pick
  4.9 0.6 fusion.36
  6.1 0.1 add_subtract_fusion
  6.2 0.1 copy.41
  6.3 0.6 compare_reduce_fusion
  6.9 0.6 fusion.10.by_shift
  7.5 0.7 gather_fusion.7
  8.1 0.7 gather_fusion.6
  8.8 0.7 gather_fusion.2
  9.5 0.7 gather_fusion
  10.2 0.7 gather_fusion.3
  10.9 0.7 gather_fusion.1
  11.6 0.6 gather_fusion.8
  12.2 0.7 concatenate.13.pick
  12.9 0.1 copy.35
  13.0 0.2 fusion.2
  13.2 0.2 dynamic-slice_reduce_fusion
  13.5 0.7 gather_fusion.4
  14.1 0.7 gather_fusion.5
  14.8 0.7 select_reduce_fusion.pair
  15.6 0.1 copy.36
  15.7 0.6 and_reduce_fusion
  16.3 0.6 iota_reduce_fusion.1
  16.9 0.7 copy.44.by_kind
  17.6 0.6 stack.2.row_pick
  18.2 0.1 copy.38
  18.3 0.1 reshape.831
  18.4 0.7 gather_fusion.9
  19.0 0.1 reshape.830
  19.1 0.1 broadcast_subtract_fusion
  19.2 0.1 sub.159
  19.3 0.1 copy.37
  19.4 0.1 add.442
  19.5 0.1 add.443
  19.6 0.6 and_select_fusion.4.turn
  20.1 0.2 reshape.751
  20.3 0.1 constant_dynamic-slice_fusion.4
  20.4 0.2 copy.47
  20.6 0.6 convert_element_type.59.fill
  21.2 0.1 copy.43
  21.3 1.3 slice.68
  22.6 1.2 fusion.1.lead_front
  23.8 279.9 %shard_map.46 = (f32[1536,256]{1,0:T(8,128)}, bf16[4,8,4,6,32,128]{5,4,3,2,1,0:T(8,128)(2,1)}) custom-call(s32[30]{0:T(128)} %concatenate.13.pick, s32[32]{0:T(128)} %and_select_fusion.4.turn, s32[4,4]{1,0:T(4,128)} %select_reduce_fusion.pair, s32[2,12]{1,0:T(2,128)} %get-tuple-element.30.src_row, s32[2,12]{1,0:T(2,128)} %get-tuple-element.29.src_tile, ...), custom_call_target="tpu_custom_call" | custom-call | tf_op jit(solution)/shard_map/pallas_call | solution.py:439
  303.8 0.0 copy-start
  303.8 1.6 abs_reduce_fusion
  305.4 0.2 copy-done
  305.6 0.2 clamp_convert_fusion
  305.8 0.1 fusion.34
  305.9 0.8 pad_add_fusion.1.right
  306.8 1.1 copy.45.left
  307.8 87.5 %shard_map.47 = f32[16384,128]{1,0:T(8,128)} custom-call(f32[128]{0:T(128)} %convert_element_type.59.fill, s32[6,16]{1,0:T(8,128)} %stack.2.row_pick, s32[4,8]{1,0:T(4,128)} %pad_add_fusion.2.col_pick, s16[128,1664]{1,0:T(8,128)(2,1)} %copy.45.left, s16[1552,128]{1,0:T(8,128)(2,1)} %pad_add_fusion.1.right, ...), custom_call_target="tpu_custom_call" | custom-call | tf_op jit(solution)/shard_map/pallas_call | solution.py:693
  395.4 7.6 %copy.55 = f32[1,16,128,1,8,128]{5,4,3,2,1,0:T(8,128)} copy(f32[1,16,128,1,8,128]{5,4,3,2,1,0:T(8,128)} %bitcast.82) | data formatting | bytes 16777216
  (38 shorter events, 0.3 us)
Async XLA Ops:
  18.4 1.8 copy-start.1
  303.8 1.9 copy-start

commit v5 on v4

--- a/solution.py
+++ b/solution.py
@@ -67,8 +67,8 @@
 CODED = NB * T
 LEFT = CODED + T
 RIGHT = CODED + 16
-X_START = (0, 2, 4, 6)
-ROW_START = (3, 6, 8, 11)
+X_START = (-1, 0, 2, 5)
+ROW_START = (1, 4, 7, 10)
 
 
 def exchange_factor_kernel(
@@ -174,6 +174,25 @@
         for d in range(1, 4):
             z_copy(q, d).start()
 
+    def x_start(q):
+        for d in range(1, 4):
+            z_copy(q, d).wait_recv()
+            if q >= 2:
+                x_copy(q - 2, d).wait_send()
+
+        @pl.loop(0, REST)
+        def _(i):
+            for kind in range(4):
+                for d in range(4):
+                    tile = z_recv[q][kind, pair[d, kind], i]
+                    if d == 0:
+                        x_recv[q][d, kind, i] = tile
+                    else:
+                        x_out[q % 2][d - 1, kind, i] = tile
+
+        for d in range(1, 4):
+            x_copy(q, d).start()
+
     @pl.loop(0, REST)
     def _(i):
         line = lax.rem(LEAD_ROWS * (first[0] + 1) + i, LEAD_ROWS + REST)
@@ -184,6 +203,9 @@
                 for d in range(1, 4):
                     z_out[q, d - 1, a, i] = tiles[line, by_kind[d, a], part]
 
+    z_start(0)
+    z_start(1)
+
     for d in range(1, n_col):
         lead_copy(d).wait()
 
@@ -196,8 +218,7 @@
             strip_copy(e, whole).start()
     strip[r] = lead_slots[r]
     corner_strip[r] = lead_slots[0]
-    z_start(0)
-    z_start(1)
+    x_start(0)
     for e in range(1, n_row):
         for whole in (False, True):
             kind, peer = int(whole), row_peer(e)
@@ -362,23 +383,7 @@
 
             @pl.when(k == X_START[q])
             def _(q=q):
-                for d in range(1, 4):
-                    z_copy(q, d).wait_recv()
-                    if q >= 2:
-                        x_copy(q - 2, d).wait_send()
-
-                @pl.loop(0, REST)
-                def _(i):
-                    for kind in range(4):
-                        for d in range(4):
-                            tile = z_recv[q][kind, pair[d, kind], i]
-                            if d == 0:
-                                x_recv[q][d, kind, i] = tile
-                            else:
-                                x_out[q % 2][d - 1, kind, i] = tile
-
-                for d in range(1, 4):
-                    x_copy(q, d).start()
+                x_start(q)
 
             @pl.when(k == ROW_START[q])
             def _(q=q):

time: 405 us -> 391 us (0.965)
  Pallas kernels: 367 us -> 350 us
    pallas_call x1, Pallas kernels: 87.5 us -> 74.7 us  [update(): pl.pallas_call(update_kernel, out_shape=jax.ShapeDtypeStruct(front.shape,...]
    pallas_call x1, Pallas kernels: 280 us -> 275 us  [exchange_factor(): pl.pallas_call(exchange_factor_kernel, out_shape=(jax.ShapeDtypeStruct((N...]
where the time goes in v5:
time: 391 us; the launch traced here: 385 us
  Pallas kernels  350 us (90%)
  local copies, waits for them, and re-layouts  23.4 us (6%)
  other arithmetic  11.2 us (3%)
    pallas_call x1, Pallas kernels, exchange_factor(): pl.pallas_call(exchange_factor_kernel, out_shape=(jax.ShapeDtypeStruct((N...  275 us
    pallas_call x1, Pallas kernels, update(): pl.pallas_call(update_kernel, out_shape=jax.ShapeDtypeStruct(front.shape,...  74.7 us
    unnamed x7, local copies, waits for them, and re-layouts  8 us

profile of v5, /device:TPU:0, one launch (start us, length us, event | category | flops | bytes accessed | tf_op | source)
XLA Modules:
  0.0 385.5 jit_solution(3022648043745993612)
XLA Ops:
  0.0 0.8 slice.57
  0.9 0.1 broadcast_compare_fusion
  1.0 0.1 fusion.32
  1.1 0.1 copy.34
  1.2 0.5 iota_reduce_fusion
  1.8 0.1 fusion.29
  1.9 0.1 copy.39
  2.0 0.8 fusion.5
  2.8 0.6 gather_fusion.10
  3.4 0.1 copy.40
  3.5 0.1 fusion.7
  3.7 0.7 and_select_fusion
  4.4 0.5 pad_add_fusion.2.col_pick
  4.9 0.6 fusion.36
  6.1 0.1 add_subtract_fusion
  6.2 0.1 copy.41
  6.3 0.6 compare_reduce_fusion
  6.9 0.6 fusion.10.by_shift
  7.5 0.7 gather_fusion.7
  8.1 0.7 gather_fusion.6
  8.8 0.7 gather_fusion.2
  9.5 0.7 gather_fusion
  10.2 0.7 gather_fusion.3
  10.9 0.7 gather_fusion.1
  11.6 0.6 gather_fusion.8
  12.2 0.7 concatenate.13.pick
  12.9 0.1 copy.35
  13.0 0.2 fusion.2
  13.2 0.2 dynamic-slice_reduce_fusion
  13.5 0.7 gather_fusion.4
  14.1 0.7 gather_fusion.5
  14.8 0.7 select_reduce_fusion.pair
  15.6 0.1 copy.36
  15.7 0.6 and_reduce_fusion
  16.3 0.6 iota_reduce_fusion.1
  16.9 0.7 copy.44.by_kind
  17.6 0.6 stack.2.row_pick
  18.2 0.1 copy.38
  18.3 0.1 reshape.831
  18.4 0.7 gather_fusion.9
  19.0 0.1 reshape.830
  19.1 0.1 broadcast_subtract_fusion
  19.2 0.1 sub.159
  19.3 0.1 copy.37
  19.4 0.1 add.442
  19.5 0.1 add.443
  19.6 0.6 and_select_fusion.4.turn
  20.1 0.0 copy-done.1
  20.1 0.2 reshape.751
  20.3 0.1 constant_dynamic-slice_fusion.4
  20.4 0.2 copy.47
  20.6 0.6 convert_element_type.59.fill
  21.2 0.1 copy.43
  21.3 1.3 slice.68
  22.6 1.2 fusion.1.lead_front
  23.8 275.2 %shard_map.46 = (f32[1536,256]{1,0:T(8,128)}, bf16[4,8,4,6,32,128]{5,4,3,2,1,0:T(8,128)(2,1)}) custom-call(s32[30]{0:T(128)} %concatenate.13.pick, s32[32]{0:T(128)} %and_select_fusion.4.turn, s32[4,4]{1,0:T(4,128)} %select_reduce_fusion.pair, s32[2,12]{1,0:T(2,128)} %get-tuple-element.30.src_row, s32[2,12]{1,0:T(2,128)} %get-tuple-element.29.src_tile, ...), custom_call_target="tpu_custom_call" | custom-call | tf_op jit(solution)/shard_map/pallas_call | solution.py:444
  299.1 1.6 abs_reduce_fusion
  300.7 0.2 copy-done
  300.9 0.2 clamp_convert_fusion
  301.1 0.1 fusion.34
  301.2 0.8 pad_add_fusion.1.right
  302.1 1.1 copy.45.left
  303.1 74.7 %shard_map.47 = f32[16384,128]{1,0:T(8,128)} custom-call(f32[128]{0:T(128)} %convert_element_type.59.fill, s32[6,16]{1,0:T(8,128)} %stack.2.row_pick, s32[4,8]{1,0:T(4,128)} %pad_add_fusion.2.col_pick, s16[128,1664]{1,0:T(8,128)(2,1)} %copy.45.left, s16[1552,128]{1,0:T(8,128)(2,1)} %pad_add_fusion.1.right, ...), custom_call_target="tpu_custom_call" | custom-call | tf_op jit(solution)/shard_map/pallas_call | solution.py:698
  377.9 7.6 %copy.55 = f32[1,16,128,1,8,128]{5,4,3,2,1,0:T(8,128)} copy(f32[1,16,128,1,8,128]{5,4,3,2,1,0:T(8,128)} %bitcast.82) | data formatting | bytes 16777216
  (38 shorter events, 0.3 us)
Async XLA Ops:
  18.4 1.8 copy-start.1
  299.1 1.9 copy-start

commit v6 on v5

--- a/solution.py
+++ b/solution.py
@@ -33,11 +33,12 @@
         for j in range(8):
             pivot = jnp.broadcast_to(cols[j][j : j + 1, :], (8, T))
             root = lax.rsqrt(pivot)
-            root = root * (1.5 - 0.5 * pivot * root * root)
-            scale = jnp.where(sub == j, root, scale)
+            miss = 1.0 - (pivot * root) * root
+            scale = jnp.where(sub == j, root + root * (0.5 * miss), scale)
             if j == 7:
                 break
-            factor = jnp.where(sub > j, cols[j] * (root * root), 0.0)
+            square = root * root
+            factor = jnp.where(sub > j, cols[j], 0.0) * (square + square * miss)
             pa = pa - factor * jnp.broadcast_to(pa[j : j + 1, :], (8, T))
             pw = pw - factor * jnp.broadcast_to(pw[j : j + 1, :], (8, T))
             for m in range(j + 1, 8):
@@ -205,6 +206,7 @@
 
     z_start(0)
     z_start(1)
+    mat[...] = jnp.zeros_like(mat)
 
     for d in range(1, n_col):
         lead_copy(d).wait()
@@ -264,15 +266,22 @@
     def ring_copy(block, part, target):
         ref = piece(block, part, core)
         copy = remote(ref, ref, ring_send.at[len(ring)], ring_got.at[block, part], {"col": target})
-        copy.start()
-        ring.append(copy)
+        ring.append((copy, block))
+
+        @pl.when(block < NB)
+        def _():
+            copy.start()
 
     def ring_wait(block, part):
         ref = piece(block, part, core)
-        remote(ref, ref, ring_send.at[0], ring_got.at[block, part], {"col": at_col(1, 0)}).wait_recv()
+        landed = remote(ref, ref, ring_send.at[0], ring_got.at[block, part], {"col": at_col(1, 0)})
         copy = remote(ref, ref, twin_send.at[len(twins)], twin_got.at[block, part], {"row": twin})
-        copy.start()
-        twins.append(copy)
+        twins.append((copy, block))
+
+        @pl.when(block < NB)
+        def _():
+            landed.wait_recv()
+            copy.start()
 
     for part in range(2):
         ring_copy(c, part, place(part, 1, 0))
@@ -313,7 +322,6 @@
 
     z_start(2)
     z_start(3)
-    mat[...] = jnp.zeros_like(mat)
     mat[:, NB * T : NB * T + T] = mine[...]
 
     @pl.when(jnp.logical_not(moves))
@@ -326,7 +334,8 @@
                 for part in range(2):
                     block = at_col(dx, dz)
                     ref = piece(block, part, 1 - core)
-                    remote(ref, ref, twin_send.at[0], twin_got.at[block, part], {"row": twin}).wait_recv()
+                    landed = remote(ref, ref, twin_send.at[0], twin_got.at[block, part], {"row": twin})
+                    pl.when(block < NB)(landed.wait_recv)
 
     for d in range(NB):
         for i in range(d, NB):
@@ -412,8 +421,8 @@
         for whole in (False, True):
             front_copy(e, whole).wait_send()
             strip_copy(e, whole).wait_send()
-    for copy in ring + twins:
-        copy.wait_send()
+    for copy, block in ring + twins:
+        pl.when(block < NB)(copy.wait_send)
     for q in range(Q):
         for d in range(1, 4):
             z_copy(q, d).wait_send()

time: 391 us -> 389 us (level)
  no operation moved by 1% of the time
where the time goes in v6:
time: 389 us; the launch traced here: 386 us
  Pallas kernels  351 us (90%)
  local copies, waits for them, and re-layouts  23.4 us (6%)
  other arithmetic  11.2 us (3%)
    pallas_call x1, Pallas kernels, exchange_factor(): pl.pallas_call(exchange_factor_kernel, out_shape=(jax.ShapeDtypeStruct((N...  273 us
    pallas_call x1, Pallas kernels, update(): pl.pallas_call(update_kernel, out_shape=jax.ShapeDtypeStruct(front.shape,...  77.9 us
    unnamed x7, local copies, waits for them, and re-layouts  8 us

profile of v6, /device:TPU:0, one launch (start us, length us, event | category | flops | bytes accessed | tf_op | source)
XLA Modules:
  0.0 386.3 jit_solution(10565462104027392116)
XLA Ops:
  0.0 0.8 slice.57
  0.9 0.1 broadcast_compare_fusion
  1.0 0.1 fusion.32
  1.1 0.1 copy.34
  1.2 0.5 iota_reduce_fusion
  1.8 0.1 fusion.29
  1.9 0.1 copy.39
  2.0 0.8 fusion.5
  2.8 0.6 gather_fusion.10
  3.4 0.1 copy.40
  3.5 0.1 fusion.7
  3.7 0.7 and_select_fusion
  4.4 0.5 pad_add_fusion.2.col_pick
  4.9 0.6 fusion.36
  6.1 0.1 add_subtract_fusion
  6.2 0.1 copy.41
  6.3 0.6 compare_reduce_fusion
  6.9 0.6 fusion.10.by_shift
  7.5 0.7 gather_fusion.7
  8.1 0.7 gather_fusion.6
  8.8 0.7 gather_fusion.2
  9.5 0.7 gather_fusion
  10.2 0.7 gather_fusion.3
  10.9 0.7 gather_fusion.1
  11.6 0.6 gather_fusion.8
  12.2 0.7 concatenate.13.pick
  12.9 0.1 copy.35
  13.0 0.2 fusion.2
  13.2 0.2 dynamic-slice_reduce_fusion
  13.5 0.7 gather_fusion.4
  14.1 0.7 gather_fusion.5
  14.8 0.7 select_reduce_fusion.pair
  15.6 0.1 copy.36
  15.7 0.6 and_reduce_fusion
  16.3 0.6 iota_reduce_fusion.1
  16.9 0.7 copy.44.by_kind
  17.6 0.6 stack.2.row_pick
  18.2 0.1 copy.38
  18.3 0.1 reshape.831
  18.4 0.7 gather_fusion.9
  19.0 0.1 reshape.830
  19.1 0.1 broadcast_subtract_fusion
  19.2 0.1 sub.159
  19.3 0.1 copy.37
  19.4 0.1 add.442
  19.5 0.1 add.443
  19.6 0.6 and_select_fusion.4.turn
  20.1 0.0 copy-done.1
  20.1 0.2 reshape.751
  20.3 0.1 constant_dynamic-slice_fusion.4
  20.4 0.2 copy.47
  20.6 0.6 convert_element_type.59.fill
  21.2 0.1 copy.43
  21.3 1.3 slice.68
  22.6 1.2 fusion.1.lead_front
  23.8 272.9 %shard_map.46 = (f32[1536,256]{1,0:T(8,128)}, bf16[4,8,4,6,32,128]{5,4,3,2,1,0:T(8,128)(2,1)}) custom-call(s32[30]{0:T(128)} %concatenate.13.pick, s32[32]{0:T(128)} %and_select_fusion.4.turn, s32[4,4]{1,0:T(4,128)} %select_reduce_fusion.pair, s32[2,12]{1,0:T(2,128)} %get-tuple-element.30.src_row, s32[2,12]{1,0:T(2,128)} %get-tuple-element.29.src_tile, ...), custom_call_target="tpu_custom_call" | custom-call | tf_op jit(solution)/shard_map/pallas_call | solution.py:453
  296.8 1.6 abs_reduce_fusion
  298.4 0.2 copy-done
  298.6 0.2 clamp_convert_fusion
  298.8 0.1 fusion.34
  298.9 0.8 pad_add_fusion.1.right
  299.8 1.1 copy.45.left
  300.8 77.9 %shard_map.47 = f32[16384,128]{1,0:T(8,128)} custom-call(f32[128]{0:T(128)} %convert_element_type.59.fill, s32[6,16]{1,0:T(8,128)} %stack.2.row_pick, s32[4,8]{1,0:T(4,128)} %pad_add_fusion.2.col_pick, s16[128,1664]{1,0:T(8,128)(2,1)} %copy.45.left, s16[1552,128]{1,0:T(8,128)(2,1)} %pad_add_fusion.1.right, ...), custom_call_target="tpu_custom_call" | custom-call | tf_op jit(solution)/shard_map/pallas_call | solution.py:707
  378.7 7.6 %copy.55 = f32[1,16,128,1,8,128]{5,4,3,2,1,0:T(8,128)} copy(f32[1,16,128,1,8,128]{5,4,3,2,1,0:T(8,128)} %bitcast.82) | data formatting | bytes 16777216
  (38 shorter events, 0.3 us)
Async XLA Ops:
  18.4 1.8 copy-start.1
  296.8 1.9 copy-start
